TPU v7x, 512 devices: a whole 4x4x16 slice. The times are simulated.
512 devices in a mesh: space: 128 (over x, z, core), view: 4 (over y).
Axes of the slice: x: 4, y: 4, z: 16, core: 2. Of those that a mesh axis runs over, the one named last changes fastest.
Arguments:
- centers: float32 [3, 2097152], P(None, ('space', 'view')), may hold values from -13 to 13, as said below
- log_scales: float32 [3, 2097152], P(None, ('space', 'view')), may hold values from -5 to -3
- rotations: float32 [4, 2097152], P(None, ('space', 'view')), may hold values from 0.1 to 1.9
- opacity: float32 [2097152], P(('space', 'view')), may hold values from -1 to 6
- harmonics: float32 [3, 16, 2097152], P(None, None, ('space', 'view')), may hold values from -1.8 to 1.8
- cameras: float32 [4, 3], replicated, may hold values from -0.05 to 0.05
- send_index: int32 [128, 4, 128, 2], P('space', 'view'), may hold values from 0 to 4095, as said below
- tile_lists: int32 [128, 8, 128], P('space'), may hold values from 0 to 1023, as said below
- counts: int32 [128, 8], P('space'), may hold values from 32 to 128, as said below
- target: float32 [4, 3, 2048, 128], P('view', None, 'space'), may hold values from 0 to 1
Outputs:
- rendered: float32 [4, 3, 2048, 128], P('view', None, 'space')
- inverse_depth: float32 [4, 2048, 128], P('view', 'space')
- grad_centers: float32 [3, 2097152], P(None, ('space', 'view'))
- grad_scales: float32 [3, 2097152], P(None, ('space', 'view'))
- grad_rotations: float32 [4, 2097152], P(None, ('space', 'view'))
- grad_opacity: float32 [2097152], P(('space', 'view'))
- grad_harmonics: float32 [3, 16, 2097152], P(None, None, ('space', 'view'))
Inputs may be any that keep to these rules, and one draw needn't show every extreme that they name: `send_index`: for each owner (first two indices) the 256 entries are distinct local Gaussian numbers. `tile_lists`: for each strip the 8 lists together name every slot exactly once; a list's Gaussians come front to back in every view. `counts`: some tile has all 128 entries live. `centers`: the third row (depth) lies from 2 to 6.
All inputs are finite; a program needn't handle non-finite values.
Results may differ from a plain program's by a relative error of at most 0.0003.
Values sent between devices are 32-bit elements; how exact they have to be, the bound alone decides.
A program may use at most 64 MiB of HBM per device.

v0:
```python
import math

import jax
import jax.numpy as jnp
from jax import lax
from jax.sharding import PartitionSpec as P

TILE = 16


FOCAL_LENGTH = 512.0
LOW_PASS = 0.3
ALPHA_MAX = 0.99
SMOOTHING = 0.05
STRUCTURE_WEIGHT = 0.2
STABLE_MEAN = 0.0001
STABLE_SPREAD = 0.0009
HARMONIC_ZERO = 0.28209479177387814
HARMONIC_ONE = 0.4886025119029199
HARMONIC_TWO = [
    1.0925484305920792,
    -1.0925484305920792,
    0.31539156525252005,
    -1.0925484305920792,
    0.5462742152960396,
]
HARMONIC_THREE = [
    -0.5900435899266435,
    2.890611442640554,
    -0.4570457994644658,
    0.3731763325901154,
    -0.4570457994644658,
    1.445305721320277,
    -0.5900435899266435,
]
TAPS_RAW = [math.exp(-((offset - 5) ** 2) / 4.5) for offset in range(11)]
WINDOW_TAPS = [value / sum(TAPS_RAW) for value in TAPS_RAW]


def extended(block, sides, width):
    for axis, dim in sides:
        count = lax.axis_size(axis)
        forward = [(i, i + 1) for i in range(count - 1)]
        backward = [(target, source) for source, target in forward]
        low = lax.ppermute(
            lax.slice_in_dim(block, block.shape[dim] - width, None, axis=dim), axis, forward
        )
        high = lax.ppermute(lax.slice_in_dim(block, 0, width, axis=dim), axis, backward)
        block = jnp.concatenate([low, block, high], axis=dim)
    return block


def harmonic_basis(unit_x, unit_y, unit_z):
    square_x = unit_x * unit_x
    square_y = unit_y * unit_y
    square_z = unit_z * unit_z
    terms = [
        HARMONIC_ZERO * jnp.ones_like(unit_x),
        -HARMONIC_ONE * unit_y,
        HARMONIC_ONE * unit_z,
        -HARMONIC_ONE * unit_x,
        HARMONIC_TWO[0] * unit_x * unit_y,
        HARMONIC_TWO[1] * unit_y * unit_z,
        HARMONIC_TWO[2] * (2.0 * square_z - square_x - square_y),
        HARMONIC_TWO[3] * unit_x * unit_z,
        HARMONIC_TWO[4] * (square_x - square_y),
        HARMONIC_THREE[0] * unit_y * (3.0 * square_x - square_y),
        HARMONIC_THREE[1] * unit_x * unit_y * unit_z,
        HARMONIC_THREE[2] * unit_y * (4.0 * square_z - square_x - square_y),
        HARMONIC_THREE[3] * unit_z * (2.0 * square_z - 3.0 * square_x - 3.0 * square_y),
        HARMONIC_THREE[4] * unit_x * (4.0 * square_z - square_x - square_y),
        HARMONIC_THREE[5] * unit_z * (square_x - square_y),
        HARMONIC_THREE[6] * unit_x * (square_x - 3.0 * square_y),
    ]
    return jnp.stack(terms)


def project_view(centers, log_scales, rotations, opacity, harmonics, camera, height, columns):
    shift_x = centers[0] - camera[0]
    shift_y = centers[1] - camera[1]
    shift_z = centers[2] - camera[2]
    inverse_z = 1.0 / shift_z
    pixel_column = FOCAL_LENGTH * shift_x * inverse_z + 0.5 * columns
    pixel_row = FOCAL_LENGTH * shift_y * inverse_z + 0.5 * height
    scalar_w, axis_x, axis_y, axis_z = (rotations[0], rotations[1], rotations[2], rotations[3])
    rot_scale = 2.0 / (scalar_w * scalar_w + axis_x * axis_x + axis_y * axis_y + axis_z * axis_z)
    rotation = [
        [
            1.0 - rot_scale * (axis_y * axis_y + axis_z * axis_z),
            rot_scale * (axis_x * axis_y - scalar_w * axis_z),
            rot_scale * (axis_x * axis_z + scalar_w * axis_y),
        ],
        [
            rot_scale * (axis_x * axis_y + scalar_w * axis_z),
            1.0 - rot_scale * (axis_x * axis_x + axis_z * axis_z),
            rot_scale * (axis_y * axis_z - scalar_w * axis_x),
        ],
        [
            rot_scale * (axis_x * axis_z - scalar_w * axis_y),
            rot_scale * (axis_y * axis_z + scalar_w * axis_x),
            1.0 - rot_scale * (axis_x * axis_x + axis_y * axis_y),
        ],
    ]
    scales = jnp.exp(log_scales)
    factor = [
        [rotation[first_axis][second_axis] * scales[second_axis] for second_axis in range(3)]
        for first_axis in range(3)
    ]

    def product_entry(left_axis, right_axis):
        return (
            factor[left_axis][0] * factor[right_axis][0]
            + factor[left_axis][1] * factor[right_axis][1]
            + factor[left_axis][2] * factor[right_axis][2]
        )

    sigma_xx = product_entry(0, 0)
    sigma_xy = product_entry(0, 1)
    sigma_xz = product_entry(0, 2)
    sigma_yy = product_entry(1, 1)
    sigma_yz = product_entry(1, 2)
    sigma_zz = product_entry(2, 2)
    jacobian_a = FOCAL_LENGTH * inverse_z
    jacobian_x = -FOCAL_LENGTH * shift_x * inverse_z * inverse_z
    jacobian_y = -FOCAL_LENGTH * shift_y * inverse_z * inverse_z
    plane_a = (
        jacobian_a * jacobian_a * sigma_xx
        + 2.0 * jacobian_a * jacobian_x * sigma_xz
        + jacobian_x * jacobian_x * sigma_zz
        + LOW_PASS
    )
    plane_b = (
        jacobian_a * jacobian_a * sigma_xy
        + jacobian_a * jacobian_y * sigma_xz
        + jacobian_x * jacobian_a * sigma_yz
        + jacobian_x * jacobian_y * sigma_zz
    )
    plane_c = (
        jacobian_a * jacobian_a * sigma_yy
        + 2.0 * jacobian_a * jacobian_y * sigma_yz
        + jacobian_y * jacobian_y * sigma_zz
        + LOW_PASS
    )
    determinant = plane_a * plane_c - plane_b * plane_b
    conic_a = plane_c / determinant
    conic_b = -plane_b / determinant
    conic_c = plane_a / determinant
    opaque = jax.nn.sigmoid(opacity)
    length = jnp.sqrt(shift_x * shift_x + shift_y * shift_y + shift_z * shift_z)
    basis = harmonic_basis(shift_x / length, shift_y / length, shift_z / length)
    colors = jnp.maximum(0.0, 0.5 + jnp.sum(harmonics * basis[None], axis=1))
    return jnp.stack(
        [
            pixel_column,
            pixel_row,
            conic_a,
            conic_b,
            conic_c,
            opaque,
            colors[0],
            colors[1],
            colors[2],
            inverse_z,
        ]
    )


def composite_block(gathered, live_count, tile_ids, strip_number, upper_ones):
    list_length = gathered.shape[2]
    pixel_ids = jnp.arange(TILE * TILE)
    pixel_x = (tile_ids[:, None] * TILE + pixel_ids[None, :] % TILE).astype(jnp.float32) + 0.5
    pixel_y = (strip_number * TILE + pixel_ids // TILE).astype(jnp.float32) + 0.5
    delta_x = gathered[0][:, None, :] - pixel_x[:, :, None]
    delta_y = gathered[1][:, None, :] - pixel_y[None, :, None]
    power = (
        -0.5
        * (
            gathered[2][:, None, :] * delta_x * delta_x
            + gathered[4][:, None, :] * delta_y * delta_y
        )
        - gathered[3][:, None, :] * delta_x * delta_y
    )
    live_mask = (jnp.arange(list_length)[None, :] < live_count[:, None]).astype(jnp.float32)
    alphas = (
        jnp.minimum(ALPHA_MAX, gathered[5][:, None, :] * jnp.exp(power)) * live_mask[:, None, :]
    )
    log_keep = jnp.log(1.0 - alphas)
    log_trans = jnp.einsum("tpk,kl->tpl", log_keep, upper_ones, precision=lax.Precision.HIGHEST)
    weight = alphas * jnp.exp(log_trans)
    return jnp.einsum("tpk,ftk->ftp", weight, gathered[6:10], precision=lax.Precision.HIGHEST)


def render_strip(slot_features, lists, live_counts, strip_number, columns):
    tile_count = lists.shape[0]
    list_length = lists.shape[1]
    group = 8
    blocks = tile_count // group
    gathered = jnp.take(slot_features, lists, axis=1)
    grouped = gathered.reshape(gathered.shape[0], blocks, group, list_length).transpose(1, 0, 2, 3)
    grouped_counts = live_counts.reshape(blocks, group)
    grouped_tiles = jnp.arange(tile_count).reshape(blocks, group)
    list_ids = jnp.arange(list_length)
    upper_ones = (list_ids[:, None] < list_ids[None, :]).astype(jnp.float32)

    def block_step(operands):
        return composite_block(operands[0], operands[1], operands[2], strip_number, upper_ones)

    result = lax.map(jax.checkpoint(block_step), (grouped, grouped_counts, grouped_tiles))
    result = result.transpose(1, 0, 2, 3).reshape(4, tile_count, TILE, TILE).transpose(0, 2, 1, 3)
    return result.reshape(4, TILE, columns)


def window_blur(stack_in, rows_out):
    vertical = WINDOW_TAPS[0] * stack_in[..., 0:rows_out, :]
    for offset in range(1, 11):
        vertical = vertical + WINDOW_TAPS[offset] * stack_in[..., offset : offset + rows_out, :]
    columns = stack_in.shape[-1]
    padded = jnp.pad(vertical, [(0, 0)] * (vertical.ndim - 1) + [(5, 5)])
    result = WINDOW_TAPS[0] * padded[..., 0:columns]
    for offset in range(1, 11):
        result = result + WINDOW_TAPS[offset] * padded[..., offset : offset + columns]
    return result


def structure_map(padded_x, padded_y, rows_out):
    stacked = jnp.stack(
        [padded_x, padded_y, padded_x * padded_x, padded_y * padded_y, padded_x * padded_y]
    )
    blurred = window_blur(stacked, rows_out)
    mean_x, mean_y, second_x, second_y, second_xy = (
        blurred[0],
        blurred[1],
        blurred[2],
        blurred[3],
        blurred[4],
    )
    spread_x = second_x - mean_x * mean_x
    spread_y = second_y - mean_y * mean_y
    spread_xy = second_xy - mean_x * mean_y
    upper_part = (2.0 * mean_x * mean_y + STABLE_MEAN) * (2.0 * spread_xy + STABLE_SPREAD)
    lower_part = (mean_x * mean_x + mean_y * mean_y + STABLE_MEAN) * (
        spread_x + spread_y + STABLE_SPREAD
    )
    return upper_part / lower_part


def strip_loss(padded_x, padded_y, rows_out, first_row, height):
    structure = structure_map(padded_x, padded_y, rows_out)
    rims = (padded_x.shape[2] - TILE) // 2
    own_x = padded_x[:, :, rims : rims + TILE]
    own_y = padded_y[:, :, rims : rims + TILE]
    smooth = jnp.sqrt((own_x - own_y) ** 2 + SMOOTHING**2)
    global_rows = first_row + jnp.arange(rows_out)
    inside = ((global_rows >= 0) & (global_rows < height)).astype(jnp.float32)
    return (
        jnp.sum((1.0 - STRUCTURE_WEIGHT) * smooth)
        + STRUCTURE_WEIGHT * jnp.sum((1.0 - structure) * inside[:, None])
    ) / (TILE * TILE)


def on_device(
    centers,
    log_scales,
    rotations,
    opacity,
    harmonics,
    cameras,
    send_index,
    tile_lists,
    counts,
    target,
):
    strip_count = lax.axis_size("space")
    strip_number = lax.axis_index("space")
    height = TILE * strip_count
    columns = target.shape[-1]
    capacity = send_index.shape[-1]
    view_count = cameras.shape[0]
    chosen = send_index[0, 0].reshape(-1)

    def owner_project(centers, log_scales, rotations, opacity, harmonics):
        everyone = jax.vmap(
            lambda camera: project_view(
                centers, log_scales, rotations, opacity, harmonics, camera, height, columns
            ),
            out_axes=1,
        )(cameras)
        features = jnp.take(everyone, chosen, axis=-1)
        return features.reshape(features.shape[0], view_count, strip_count, capacity)

    outgoing, owner_pull = jax.vjp(
        owner_project, centers, log_scales, rotations, opacity, harmonics
    )
    incoming = lax.all_to_all(
        lax.all_to_all(outgoing, "space", split_axis=2, concat_axis=2, tiled=True),
        "view",
        split_axis=1,
        concat_axis=1,
        tiled=True,
    )
    slot_features = incoming.reshape(incoming.shape[0], -1)
    lists = tile_lists[0]
    live_counts = counts[0]

    def render_local(slot_features):
        return render_strip(slot_features, lists, live_counts, strip_number, columns)

    stacked, render_pull = jax.vjp(render_local, slot_features)
    rendered = stacked[:3][None]
    inverse_depth = stacked[3][None]
    both_images = jnp.concatenate([rendered, target], axis=1)
    padded_both = extended(both_images, (("space", 2),), 5)
    padded_y = padded_both[:, 3:]

    def local_loss(padded_x):
        return strip_loss(padded_x, padded_y, TILE, strip_number * TILE, height)

    grad_padded = jax.grad(local_loss)(padded_both[:, :3])
    edges = jnp.concatenate([grad_padded[:, :, :5], grad_padded[:, :, -5:]], axis=2)
    returned = extended(edges, (("space", 2),), 5)
    from_above = returned[:, :, :5]
    from_below = returned[:, :, -5:]
    grad_image = grad_padded[:, :, 5 : 5 + TILE]
    grad_image = grad_image + jnp.pad(from_above, ((0, 0), (0, 0), (0, TILE - 5), (0, 0)))
    grad_image = grad_image + jnp.pad(from_below, ((0, 0), (0, 0), (TILE - 5, 0), (0, 0)))
    cotangent = jnp.concatenate([grad_image[0], jnp.zeros_like(stacked[3:])], axis=0)
    grad_slots = render_pull(cotangent)[0]
    backward = grad_slots[:9].reshape(9, view_count, strip_count, capacity)
    returned_grads = lax.all_to_all(
        lax.all_to_all(backward, "space", split_axis=2, concat_axis=2, tiled=True),
        "view",
        split_axis=1,
        concat_axis=1,
        tiled=True,
    )
    full_grads = jnp.concatenate([returned_grads, jnp.zeros_like(outgoing[9:])], axis=0)
    grads = owner_pull(full_grads)
    return (rendered, inverse_depth, grads[0], grads[1], grads[2], grads[3], grads[4])


def solution(mesh):
    return jax.shard_map(
        on_device,
        mesh=mesh,
        in_specs=(
            P(None, ("space", "view")),
            P(None, ("space", "view")),
            P(None, ("space", "view")),
            P(("space", "view")),
            P(None, None, ("space", "view")),
            P(),
            P("space", "view", None, None),
            P("space", None, None),
            P("space", None),
            P("view", None, "space", None),
        ),
        out_specs=(
            P("view", None, "space", None),
            P("view", "space", None),
            P(None, ("space", "view")),
            P(None, ("space", "view")),
            P(None, ("space", "view")),
            P(("space", "view")),
            P(None, None, ("space", "view")),
        ),
        check_vma=False,
    )
```

profile of v0, /device:TPU:1, one launch (start us, length us, event | category | flops | bytes accessed | tf_op | source)
XLA Modules:
  0.0 238.1 jit_solution(13595085740179346636)
XLA Ops:
  1.3 0.8 copy.1421
  2.1 1.0 slice_reduce_fusion.1
  3.1 0.7 copy.1404
  3.9 1.3 add_divide_fusion
  5.2 1.0 fusion.268
  6.2 0.9 exp.22
  8.4 1.8 multiply_add_fusion.15
  10.4 1.9 multiply_add_fusion.13
  14.3 0.7 copy.1418
  15.0 0.7 copy.1414
  17.3 3.1 %stack.17 = f32[4,16,4096]{2,1,0:T(8,128)S(1)} concatenate(f32[4,1,4096]{2,1,0:T(1,128)} %broadcast_in_dim.103, f32[4,1,4096]{2,1,0:T(1,128)S(1)} %copy.1405, f32[4,1,4096]{2,1,0:T(1,128)S(1)} %copy.1406, f32[4,1,4096]{2,1,0:T(1,128)S(1)} %copy.1407, f32[4,1,4096]{2,1,0:T(1,128)} %copy.1408, f32[4,1,4096]{2,1,0:T(1,128)S(1)} %copy.1409, f32[4,1,4096]{2,1,0:T(1,128)S(1)} %copy.1410, ...), dimensions={1} | concatenate | bytes 2097152 | tf_op jit(solution)/shard_map/jvp(vmap())/stack | solution.py:75
  21.0 0.7 broadcast_dynamic-update-slice_fusion
  21.9 0.8 fusion.193
  22.7 5.9 %copy.1422 = f32[10,4,4096]{0,1,2:T(4,128)} copy(f32[10,4,4096]{2,1,0:T(4,128)S(1)} %bitcast.424) | data formatting | bytes 1310720 | tf_op jit(solution)/shard_map/jvp(vmap())/transpose | solution.py:282
  28.7 4.6 %gather_fusion = f32[256,10,4]{1,2,0:T(4,128)S(1)} fusion(f32[10,4,4096]{0,1,2:T(4,128)} %copy.1422, s32[1024]{0:T(1024)} %pad_clamp_fusion), kind=kCustom, calls=%fused_computation | custom fusion | bytes 82944 | tf_op jit(solution)/shard_map/jvp(jit(_take))/gather | solution.py:288
  33.6 1.0 copy.1424
  34.6 20.4 %all-to-all-start = ((f32[10,4,128,2]{0,3,1,2:T(2,128)}), f32[10,4,128,2]{0,3,1,2:T(2,128)S(1)}, u32[]{:S(2)}, u32[]{:S(2)}) async-start(f32[10,4,128,2]{0,3,1,2:T(2,128)} %copy.1424), calls=%async_computation | async-start | bytes 1048576 | tf_op jit(solution)/shard_map/all_to_all | solution.py:295
  55.2 33.0 %all-to-all-done = f32[10,4,128,2]{0,3,1,2:T(2,128)S(1)} async-done(((f32[10,4,128,2]{0,3,1,2:T(2,128)}), f32[10,4,128,2]{0,3,1,2:T(2,128)S(1)}, u32[]{:S(2)}, u32[]{:S(2)}) %all-to-all-start) | async-done | bytes 40992 | tf_op jit(solution)/shard_map/all_to_all | solution.py:295
  88.2 1.0 copy.1425
  89.1 4.2 %all-to-all-start.1 = ((f32[10,4,128,2]{2,3,0,1:T(2,128)}), f32[10,4,128,2]{2,3,0,1:T(2,128)S(1)}, u32[]{:S(2)}, u32[]{:S(2)}) async-start(f32[10,4,128,2]{2,3,0,1:T(2,128)} %copy.1425), calls=%async_computation.1 | async-start | bytes 81920 | tf_op jit(solution)/shard_map/all_to_all | solution.py:294
  93.3 4.3 %all-to-all-done.1 = f32[10,4,128,2]{2,3,0,1:T(2,128)S(1)} async-done(((f32[10,4,128,2]{2,3,0,1:T(2,128)}), f32[10,4,128,2]{2,3,0,1:T(2,128)S(1)}, u32[]{:S(2)}, u32[]{:S(2)}) %all-to-all-start.1) | async-done | bytes 40992 | tf_op jit(solution)/shard_map/all_to_all | solution.py:294
  97.9 2.8 %gather_fusion.1 = f32[1024,10]{1,0:T(8,128)S(1)} fusion(f32[10,1024]{0,1:T(8,128)S(1)} %bitcast.388, s32[1024]{0:T(1024)S(1)} %broadcast_clamp_fusion), kind=kCustom, calls=%fused_computation.1 | custom fusion | bytes 86016 | tf_op jit(solution)/shard_map/jvp(jit(_take))/gather | solution.py:198
  101.0 1.7 fusion.5
  102.7 1.0 convolution_bitcast_fusion
  104.1 6.2 %collective-permute-start = (f32[1,6,5,128]{3,2,1,0:T(8,128)S(1)}, f32[1,6,5,128]{3,2,1,0:T(8,128)S(1)}, u32[]{:S(2)}, u32[]{:S(2)}) collective-permute-start(f32[1,6,5,128]{3,2,1,0:T(8,128)S(1)} %get-tuple-element.223), channel_id=1, source_target_pairs={{0,4},{4,8},{8,12},{12,16},{16,20},{20,24},{24,28},{28,32},{32,36}... | collective-permute-start | bytes 46088 | tf_op jit(solution)/shard_map/ppermute | solution.py:45
  110.3 1.9 collective-permute-start.1
  112.3 3.2 %collective-permute-done.1 = f32[1,6,5,128]{3,2,1,0:T(8,128)S(1)} collective-permute-done((f32[1,6,5,128]{3,2,1,0:T(8,128)S(1)}, f32[1,6,5,128]{3,2,1,0:T(8,128)S(1)}, u32[]{:S(2)}, u32[]{:S(2)}) %collective-permute-start.1) | collective-permute-done | bytes 15392 | tf_op jit(solution)/shard_map/ppermute | solution.py:48
  117.3 1.9 collective-permute-start.2
  119.2 2.4 %collective-permute-start.3 = (f32[1,3,5,128]{3,2,1,0:T(8,128)S(1)}, f32[1,3,5,128]{3,2,1,0:T(8,128)S(1)}, u32[]{:S(2)}, u32[]{:S(2)}) collective-permute-start(f32[1,3,5,128]{3,2,1,0:T(8,128)S(1)} %get-tuple-element.222), channel_id=1, source_target_pairs={{4,0},{8,4},{12,8},{16,12},{20,16},{24,20},{28,24},{32,28},{36,32}... | collective-permute-start | bytes 23048 | tf_op jit(solution)/shard_map/ppermute | solution.py:48
  121.7 2.6 %collective-permute-done.3 = f32[1,3,5,128]{3,2,1,0:T(8,128)S(1)} collective-permute-done((f32[1,3,5,128]{3,2,1,0:T(8,128)S(1)}, f32[1,3,5,128]{3,2,1,0:T(8,128)S(1)}, u32[]{:S(2)}, u32[]{:S(2)}) %collective-permute-start.3) | collective-permute-done | bytes 7712 | tf_op jit(solution)/shard_map/ppermute | solution.py:48
  124.8 1.9 fusion.189
  126.8 1.6 convolution_exponential_fusion
  128.3 1.3 convolution_bitcast_fusion.1
  129.6 3.4 %fusion.25 = (f32[8,128]{1,0:T(8,128)S(1)}, f32[8,128]{1,0:T(8,128)S(1)}, f32[8,128]{1,0:T(8,128)S(1)}, f32[8,128]{1,0:T(8,128)S(1)}, f32[8,128]{1,0:T(8,128)S(1)}, /*index=5*/f32[8,128]{1,0:T(8,128)S(1)}) fusion(f32[256]{0:T(256)S(1)} %convert_add_fusion.2, f32[8,128]{1,0:T(8,128)S(1)} %bitcast.462, f32[8,256]{1,0:T(8,128)S(1)} %convert_add_fusion, ...), kind=kOutput, calls=%fused_computation.55 | convolution fusion | flops 420472832 | bytes 2225152 | tf_op jit(solution)/shard_map/transpose(jvp())/while/body/eval_jaxpr/checkpoint/tpk,kl->tpl/dot_general | solution.py:188
  133.0 1.0 copy.1447
  134.1 6.5 %scatter_custom_fusion = f32[10,1024]{0,1:T(8,128)S(1)} fusion(s32[1024]{0:T(1024)S(1)} %fusion.219, f32[1024,10]{1,0:T(8,128)} %bitcast.442, f32[]{:T(128)} %constant.132.clone.1), kind=kCustom, calls=%fused_computation.101 | custom fusion | flops 10240 | bytes 41472 | tf_op jit(solution)/shard_map/transpose(jvp(jit(_take)))/scatter-add | solution.py:198
  140.8 42.9 %all_to_all.20 = f32[9,4,128,2]{0,3,1,2:T(2,128)S(1)} all-to-all(f32[9,4,128,2]{0,3,1,2:T(2,128)S(1)} %copy.1434), channel_id=1, replica_groups=mesh['space'=128,'view'=4] {'space'}, dimensions={2} | all-to-all | bytes 73728 | tf_op jit(solution)/shard_map/all_to_all | solution.py:330
  183.7 1.0 copy.1435
  184.7 3.5 %all-to-all-start.3 = ((f32[9,4,128,2]{2,3,0,1:T(2,128)}), f32[9,4,128,2]{2,3,0,1:T(2,128)S(1)}, u32[]{:S(2)}, u32[]{:S(2)}) async-start(f32[9,4,128,2]{2,3,0,1:T(2,128)} %copy.1435), calls=%async_computation.3 | async-start | bytes 73728 | tf_op jit(solution)/shard_map/all_to_all | solution.py:329
  188.9 3.3 %all-to-all-done.3 = f32[9,4,128,2]{2,3,0,1:T(2,128)S(1)} async-done(((f32[9,4,128,2]{2,3,0,1:T(2,128)}), f32[9,4,128,2]{2,3,0,1:T(2,128)S(1)}, u32[]{:S(2)}, u32[]{:S(2)}) %all-to-all-start.3) | async-done | bytes 36896 | tf_op jit(solution)/shard_map/all_to_all | solution.py:329
  193.1 3.9 %broadcast_in_dim.158 = f32[10,4,4096]{0,1,2:T(4,128)} broadcast(f32[]{:T(128)} %constant.132.clone.1), dimensions={} | broadcast | bytes 655364 | tf_op jit(solution)/shard_map/transpose(jvp(jit(_take)))/broadcast_in_dim | solution.py:288
  196.9 25.0 %scatter_fusion = f32[10,4,4096]{0,1,2:T(4,128)} fusion(f32[10,4,4096]{0,1,2:T(4,128)} %broadcast_in_dim.158, s32[256]{0:T(256)S(1)} %bitcast.453, f32[256,10,4]{1,2,0:T(4,128)S(1)} %copy.1437), kind=kCustom, calls=%fused_computation.3 | custom fusion | flops 10240 | bytes 123904 | tf_op jit(solution)/shard_map/transpose(jvp(jit(_take)))/scatter-add | solution.py:288
  222.0 6.7 %copy.1438 = f32[10,4,4096]{2,1,0:T(4,128)S(1)} copy(f32[10,4,4096]{0,1,2:T(4,128)} %scatter_fusion) | data formatting | bytes 1310720 | tf_op jit(solution)/shard_map/transpose(jvp(jit(_take)))/scatter-add | solution.py:288
  230.1 1.3 multiply_reduce_fusion
  231.6 1.0 fusion.265
  232.6 1.6 fusion.184
  234.2 0.9 fusion.120
  237.3 0.8 add_multiply_fusion
  (179 shorter events, 15.3 us)
Async XLA Ops:
  3.1 13.5 %copy-start.25 = (f32[4]{0:T(128)}, f32[4]{0:T(128)S(1)}, u32[]{:S(2)}) copy-start(f32[4]{0:T(128)S(1)} %get-tuple-element.92) | copy-start | bytes 52
  3.1 13.5 %copy-start.28 = (f32[4]{0:T(128)}, f32[4]{0:T(128)S(1)}, u32[]{:S(2)}) copy-start(f32[4]{0:T(128)S(1)} %get-tuple-element.90) | copy-start | bytes 52
  3.1 13.5 %copy-start.30 = (f32[4]{0:T(128)}, f32[4]{0:T(128)S(1)}, u32[]{:S(2)}) copy-start(f32[4]{0:T(128)S(1)} %get-tuple-element.91) | copy-start | bytes 52
  7.2 0.6 copy-start.33
  10.2 2.1 copy-start.10
  10.2 2.1 copy-start.12
  10.2 2.1 copy-start.14
  10.4 10.0 %copy-start = (f32[3,16,4096]{2,1,0:T(8,128)S(1)}, f32[3,16,4096]{2,1,0:T(8,128)}, u32[]{:S(2)}) copy-start(f32[3,16,4096]{2,1,0:T(8,128)} %param.14) | copy-start | bytes 2359300
  12.3 1.4 copy-start.4
  12.3 1.4 copy-start.6
  12.3 1.4 copy-start.8
  22.7 10.6 %copy-start.16 = (pred[128,2]{1,0:T(8,128)(4,1)S(1)}, pred[128,2]{1,0:T(8,128)(4,1)}, u32[]{:S(2)}) copy-start(pred[128,2]{1,0:T(8,128)(4,1)} %copy.1404) | copy-start | bytes 772
  28.7 26.3 %copy-start.27 = (s32[1,8,128]{2,1,0:T(8,128)S(1)}, s32[1,8,128]{2,1,0:T(8,128)}, u32[]{:S(2)}) copy-start(s32[1,8,128]{2,1,0:T(8,128)} %param.17) | copy-start | bytes 12292
  28.7 26.5 %copy-start.35 = (s32[1,8]{1,0:T(1,128)S(1)}, s32[1,8]{1,0:T(1,128)}, u32[]{:S(2)}) copy-start(s32[1,8]{1,0:T(1,128)} %param.18) | copy-start | bytes 100
  34.6 53.6 %all-to-all-start = ((f32[10,4,128,2]{0,3,1,2:T(2,128)}), f32[10,4,128,2]{0,3,1,2:T(2,128)S(1)}, u32[]{:S(2)}, u32[]{:S(2)}) async-start(f32[10,4,128,2]{0,3,1,2:T(2,128)} %copy.1424), calls=%async_computation | async-start | bytes 1048576 | tf_op jit(solution)/shard_map/all_to_all | solution.py:295
  89.1 8.5 %all-to-all-start.1 = ((f32[10,4,128,2]{2,3,0,1:T(2,128)}), f32[10,4,128,2]{2,3,0,1:T(2,128)S(1)}, u32[]{:S(2)}, u32[]{:S(2)}) async-start(f32[10,4,128,2]{2,3,0,1:T(2,128)} %copy.1425), calls=%async_computation.1 | async-start | bytes 81920 | tf_op jit(solution)/shard_map/all_to_all | solution.py:294
  101.0 3.1 %copy-start.32 = (f32[1,3,16,128]{3,2,1,0:T(8,128)S(1)}, f32[1,3,16,128]{3,2,1,0:T(8,128)}, u32[]{:S(2)}) copy-start(f32[1,3,16,128]{3,2,1,0:T(8,128)} %param.19) | copy-start | bytes 73732
  104.0 13.0 %copy-start.3 = (f32[1,3,16,128]{3,2,1,0:T(8,128)}, f32[1,3,16,128]{3,2,1,0:T(8,128)S(1)}, u32[]{:S(2)}) copy-start(f32[1,3,16,128]{3,2,1,0:T(8,128)S(1)} %broadcast_in_dim.157) | copy-start | bytes 73732
  104.1 8.2 %collective-permute-start = (f32[1,6,5,128]{3,2,1,0:T(8,128)S(1)}, f32[1,6,5,128]{3,2,1,0:T(8,128)S(1)}, u32[]{:S(2)}, u32[]{:S(2)}) collective-permute-start(f32[1,6,5,128]{3,2,1,0:T(8,128)S(1)} %get-tuple-element.223), channel_id=1, source_target_pairs={{0,4},{4,8},{8,12},{12,16},{16,20},{20,24},{24,28},{28,32},{32,36}... | collective-permute-start | bytes 46088 | tf_op jit(solution)/shard_map/ppermute | solution.py:45
  110.3 5.1 %collective-permute-start.1 = (f32[1,6,5,128]{3,2,1,0:T(8,128)S(1)}, f32[1,6,5,128]{3,2,1,0:T(8,128)S(1)}, u32[]{:S(2)}, u32[]{:S(2)}) collective-permute-start(f32[1,6,5,128]{3,2,1,0:T(8,128)S(1)} %get-tuple-element.224), channel_id=1, source_target_pairs={{4,0},{8,4},{12,8},{16,12},{20,16},{24,20},{28,24},{32,28},{36,32}... | collective-permute-start | bytes 46088 | tf_op jit(solution)/shard_map/ppermute | solution.py:48
  117.3 4.4 %collective-permute-start.2 = (f32[1,3,5,128]{3,2,1,0:T(8,128)S(1)}, f32[1,3,5,128]{3,2,1,0:T(8,128)S(1)}, u32[]{:S(2)}, u32[]{:S(2)}) collective-permute-start(f32[1,3,5,128]{3,2,1,0:T(8,128)S(1)} %get-tuple-element.221), channel_id=1, source_target_pairs={{0,4},{4,8},{8,12},{12,16},{16,20},{20,24},{24,28},{28,32},{32,36}... | collective-permute-start | bytes 23048 | tf_op jit(solution)/shard_map/ppermute | solution.py:45
  119.2 5.0 %collective-permute-start.3 = (f32[1,3,5,128]{3,2,1,0:T(8,128)S(1)}, f32[1,3,5,128]{3,2,1,0:T(8,128)S(1)}, u32[]{:S(2)}, u32[]{:S(2)}) collective-permute-start(f32[1,3,5,128]{3,2,1,0:T(8,128)S(1)} %get-tuple-element.222), channel_id=1, source_target_pairs={{4,0},{8,4},{12,8},{16,12},{20,16},{24,20},{28,24},{32,28},{36,32}... | collective-permute-start | bytes 23048 | tf_op jit(solution)/shard_map/ppermute | solution.py:48
  184.7 7.6 %all-to-all-start.3 = ((f32[9,4,128,2]{2,3,0,1:T(2,128)}), f32[9,4,128,2]{2,3,0,1:T(2,128)S(1)}, u32[]{:S(2)}, u32[]{:S(2)}) async-start(f32[9,4,128,2]{2,3,0,1:T(2,128)} %copy.1435), calls=%async_computation.3 | async-start | bytes 73728 | tf_op jit(solution)/shard_map/all_to_all | solution.py:329
  193.1 3.9 %copy-start.34 = (s32[256,1]{0,1:T(1,128)S(1)}, s32[256,1]{0,1:T(1,128)}, u32[]{:S(2)}) copy-start(s32[256,1]{0,1:T(1,128)} %copy-done.33) | copy-start | bytes 3076
  222.0 6.8 %copy-start.26 = (f32[4]{0:T(128)S(1)}, f32[4]{0:T(128)}, u32[]{:S(2)}) copy-start(f32[4]{0:T(128)} %copy-done.25) | copy-start | bytes 52
  222.0 6.8 %copy-start.29 = (f32[4]{0:T(128)S(1)}, f32[4]{0:T(128)}, u32[]{:S(2)}) copy-start(f32[4]{0:T(128)} %copy-done.28) | copy-start | bytes 52
  222.0 6.8 %copy-start.31 = (f32[4]{0:T(128)S(1)}, f32[4]{0:T(128)}, u32[]{:S(2)}) copy-start(f32[4]{0:T(128)} %copy-done.30) | copy-start | bytes 52
  222.0 7.1 %copy-start.21 = (f32[4096]{0:T(1024)S(1)}, f32[4096]{0:T(1024)}, u32[]{:S(2)}) copy-start(f32[4096]{0:T(1024)} %param.13) | copy-start | bytes 49156
  231.4 3.7 %copy-start.1 = (f32[4,4096]{1,0:T(4,128)S(1)}, f32[4,4096]{1,0:T(4,128)}, u32[]{:S(2)}) copy-start(f32[4,4096]{1,0:T(4,128)} %param.12) | copy-start | bytes 196612
  231.4 3.7 %copy-start.5 = (f32[1,4096]{1,0:T(1,128)S(1)}, f32[1,4096]{1,0:T(1,128)}, u32[]{:S(2)}) copy-start(f32[1,4096]{1,0:T(1,128)} %copy-done.4) | copy-start | bytes 49156
  231.4 3.7 %copy-start.7 = (f32[1,4096]{1,0:T(1,128)S(1)}, f32[1,4096]{1,0:T(1,128)}, u32[]{:S(2)}) copy-start(f32[1,4096]{1,0:T(1,128)} %copy-done.6) | copy-start | bytes 49156
  231.4 3.7 %copy-start.9 = (f32[1,4096]{1,0:T(1,128)S(1)}, f32[1,4096]{1,0:T(1,128)}, u32[]{:S(2)}) copy-start(f32[1,4096]{1,0:T(1,128)} %copy-done.8) | copy-start | bytes 49156
  231.4 3.7 %copy-start.11 = (f32[1,4096]{1,0:T(1,128)S(1)}, f32[1,4096]{1,0:T(1,128)}, u32[]{:S(2)}) copy-start(f32[1,4096]{1,0:T(1,128)} %copy-done.10) | copy-start | bytes 49156
  231.5 3.7 %copy-start.13 = (f32[1,4096]{1,0:T(1,128)S(1)}, f32[1,4096]{1,0:T(1,128)}, u32[]{:S(2)}) copy-start(f32[1,4096]{1,0:T(1,128)} %copy-done.12) | copy-start | bytes 49156
  231.5 3.7 %copy-start.15 = (f32[1,4096]{1,0:T(1,128)S(1)}, f32[1,4096]{1,0:T(1,128)}, u32[]{:S(2)}) copy-start(f32[1,4096]{1,0:T(1,128)} %copy-done.14) | copy-start | bytes 49156
  231.5 3.7 %copy-start.24 = (f32[1,4096]{1,0:T(1,128)S(1)}, f32[1,4096]{1,0:T(1,128)}, u32[]{:S(2)}) copy-start(f32[1,4096]{1,0:T(1,128)} %get-tuple-element.135) | copy-start | bytes 49156
  231.5 4.9 %copy-start.23 = (f32[1,4096]{1,0:T(1,128)S(1)}, f32[1,4096]{1,0:T(1,128)}, u32[]{:S(2)}) copy-start(f32[1,4096]{1,0:T(1,128)} %get-tuple-element.131) | copy-start | bytes 49156
  231.5 4.9 %copy-start.22 = (f32[1,4096]{1,0:T(1,128)S(1)}, f32[1,4096]{1,0:T(1,128)}, u32[]{:S(2)}) copy-start(f32[1,4096]{1,0:T(1,128)} %get-tuple-element.133) | copy-start | bytes 49156
  231.5 5.0 %copy-start.20 = (f32[1,4096]{1,0:T(1,128)S(1)}, f32[1,4096]{1,0:T(1,128)}, u32[]{:S(2)}) copy-start(f32[1,4096]{1,0:T(1,128)} %get-tuple-element.144) | copy-start | bytes 49156
  231.5 5.0 %copy-start.19 = (f32[1,4096]{1,0:T(1,128)S(1)}, f32[1,4096]{1,0:T(1,128)}, u32[]{:S(2)}) copy-start(f32[1,4096]{1,0:T(1,128)} %get-tuple-element.147) | copy-start | bytes 49156
  231.5 5.0 %copy-start.18 = (f32[1,4096]{1,0:T(1,128)S(1)}, f32[1,4096]{1,0:T(1,128)}, u32[]{:S(2)}) copy-start(f32[1,4096]{1,0:T(1,128)} %get-tuple-element.172) | copy-start | bytes 49156
  231.5 5.0 %copy-start.17 = (f32[1,4096]{1,0:T(1,128)S(1)}, f32[1,4096]{1,0:T(1,128)}, u32[]{:S(2)}) copy-start(f32[1,4096]{1,0:T(1,128)} %get-tuple-element.170) | copy-start | bytes 49156
  231.5 5.8 %copy-start.2 = (f32[3,4096]{1,0:T(4,128)S(1)}, f32[3,4096]{1,0:T(4,128)}, u32[]{:S(2)}) copy-start(f32[3,4096]{1,0:T(4,128)} %param.11) | copy-start | bytes 147460
where the time goes:
time: 241 us; the launch traced here: 238 us
  other arithmetic  51.1 us (21%)
  waiting for transfers between devices  46.4 us (19%)
  local copies, waits for them, and re-layouts  44.5 us (18%)
  blocking collectives  42.9 us (18%)
  starting transfers between devices  40.5 us (17%)
  matrix products  10.8 us (4%)
    all_to_all x1, blocking collectives, on_device(): lax.all_to_all(backward, 'space', split_axis=2, concat_axis=2, tiled=True)  42.9 us
    all_to_all x1, waiting for transfers between devices, on_device(): lax.all_to_all(outgoing, 'space', split_axis=2, concat_axis=2, tiled=True)  33 us
    scatter-add x1, other arithmetic, owner_project(): features = jnp.take(everyone, chosen, axis=-1)  25 us
    all_to_all x1, starting transfers between devices, on_device(): lax.all_to_all(outgoing, 'space', split_axis=2, concat_axis=2, tiled=True)  20.4 us
    ppermute x2, starting transfers between devices, extended(): lax.ppermute(lax.slice_in_dim(block, block.shape[dim] - width, None, axis...  8.15 us
    scatter-add x1, local copies, waits for them, and re-layouts, owner_project(): features = jnp.take(everyone, chosen, axis=-1)  6.73 us
    dot_general x3, matrix products, composite_block(): jnp.einsum('tpk,kl->tpl', log_keep, upper_ones, precision=lax.Precision.H...  6.63 us
    scatter-add x1, other arithmetic, render_strip(): gathered = jnp.take(slot_features, lists, axis=1)  6.54 us
  transfers between devices with their start and end apart: 7, of which 5 were waited for; matrix products, arithmetic and copies ran while one was open for 0% of the time, Pallas kernels for 0%

commit v1 on v0

v1 whole, which is shorter than its diff:
```python
import functools
import math

import jax
import jax.numpy as jnp
from jax import lax
from jax.experimental import pallas as pl
from jax.experimental.pallas import tpu as pltpu
from jax.sharding import PartitionSpec as P

TILE = 16
FOCAL_LENGTH = 512.0
LOW_PASS = 0.3
ALPHA_MAX = 0.99
SMOOTHING = 0.05
STRUCTURE_WEIGHT = 0.2
STABLE_MEAN = 0.0001
STABLE_SPREAD = 0.0009
HARMONIC_ZERO = 0.28209479177387814
HARMONIC_ONE = 0.4886025119029199
HARMONIC_TWO = [
    1.0925484305920792,
    -1.0925484305920792,
    0.31539156525252005,
    -1.0925484305920792,
    0.5462742152960396,
]
HARMONIC_THREE = [
    -0.5900435899266435,
    2.890611442640554,
    -0.4570457994644658,
    0.3731763325901154,
    -0.4570457994644658,
    1.445305721320277,
    -0.5900435899266435,
]
TAPS_RAW = [math.exp(-((offset - 5) ** 2) / 4.5) for offset in range(11)]
WINDOW_TAPS = [value / sum(TAPS_RAW) for value in TAPS_RAW]

F32 = jnp.float32
BF16 = jnp.bfloat16
MESH = pl.DeviceIdType.MESH
VMEM = pltpu.VMEM
EXACT = lax.Precision.HIGHEST


def harmonic_basis(ux, uy, uz):
    xx, yy, zz = ux * ux, uy * uy, uz * uz
    return [
        HARMONIC_ZERO * jnp.ones_like(ux),
        -HARMONIC_ONE * uy,
        HARMONIC_ONE * uz,
        -HARMONIC_ONE * ux,
        HARMONIC_TWO[0] * ux * uy,
        HARMONIC_TWO[1] * uy * uz,
        HARMONIC_TWO[2] * (2.0 * zz - xx - yy),
        HARMONIC_TWO[3] * ux * uz,
        HARMONIC_TWO[4] * (xx - yy),
        HARMONIC_THREE[0] * uy * (3.0 * xx - yy),
        HARMONIC_THREE[1] * ux * uy * uz,
        HARMONIC_THREE[2] * uy * (4.0 * zz - xx - yy),
        HARMONIC_THREE[3] * uz * (2.0 * zz - 3.0 * xx - 3.0 * yy),
        HARMONIC_THREE[4] * ux * (4.0 * zz - xx - yy),
        HARMONIC_THREE[5] * uz * (xx - yy),
        HARMONIC_THREE[6] * ux * (xx - 3.0 * yy),
    ]


def project(harmonics, center, log_scale, quaternion, opacity, camera, height, columns):
    tx, ty, tz = (center[i] - camera[i] for i in range(3))
    iz = 1.0 / tz
    u = FOCAL_LENGTH * tx * iz + 0.5 * columns
    r = FOCAL_LENGTH * ty * iz + 0.5 * height
    qw, qx, qy, qz = quaternion
    s = 2.0 / (qw * qw + qx * qx + qy * qy + qz * qz)
    rot = [
        [1.0 - s * (qy * qy + qz * qz), s * (qx * qy - qw * qz), s * (qx * qz + qw * qy)],
        [s * (qx * qy + qw * qz), 1.0 - s * (qx * qx + qz * qz), s * (qy * qz - qw * qx)],
        [s * (qx * qz - qw * qy), s * (qy * qz + qw * qx), 1.0 - s * (qx * qx + qy * qy)],
    ]
    scales = [jnp.exp(v) for v in log_scale]
    m = [[rot[i][j] * scales[j] for j in range(3)] for i in range(3)]

    def entry(i, j):
        return m[i][0] * m[j][0] + m[i][1] * m[j][1] + m[i][2] * m[j][2]

    ja = FOCAL_LENGTH * iz
    jx = -FOCAL_LENGTH * tx * iz * iz
    jy = -FOCAL_LENGTH * ty * iz * iz
    sxz, syz, szz = entry(0, 2), entry(1, 2), entry(2, 2)
    pa = ja * ja * entry(0, 0) + 2.0 * ja * jx * sxz + jx * jx * szz + LOW_PASS
    pb = ja * ja * entry(0, 1) + ja * jy * sxz + jx * ja * syz + jx * jy * szz
    pc = ja * ja * entry(1, 1) + 2.0 * ja * jy * syz + jy * jy * szz + LOW_PASS
    det = pa * pc - pb * pb
    opaque = 1.0 / (1.0 + jnp.exp(-opacity))
    length = jnp.sqrt(tx * tx + ty * ty + tz * tz)
    basis = harmonic_basis(tx / length, ty / length, tz / length)
    colors = []
    for ch in range(3):
        total = harmonics[ch * 16] * basis[0]
        for i in range(1, 16):
            total = total + harmonics[ch * 16 + i] * basis[i]
        colors.append(jnp.maximum(0.0, 0.5 + total))
    return [u, r, pc / det, -pb / det, pa / det, opaque, colors[0], colors[1], colors[2], iz]


def iota(shape, dim):
    return lax.broadcasted_iota(jnp.int32, shape, dim)


def one_hot(condition):
    return jnp.where(condition, 1.0, 0.0).astype(BF16)


def split(value, parts):
    out = []
    for _ in range(parts - 1):
        high = value.astype(BF16)
        out.append(high)
        value = value - high.astype(F32)
    out.append(value.astype(BF16))
    return out


def dot(a, b):
    return jnp.dot(a, b, preferred_element_type=F32)


def dot_exact(a, b):
    return jnp.dot(a, b, preferred_element_type=F32, precision=EXACT)


def view_camera(cam_ref):
    view = iota((8, 128), 0) // 2
    out = []
    for i in range(3):
        value = jnp.full((8, 128), cam_ref[3, i], F32)
        for v in range(3):
            value = jnp.where(view == v, cam_ref[v, i], value)
        out.append(value)
    return out


def spread_params(gp):
    odd = iota((8, 128), 0) % 2
    return [
        jnp.where(
            odd == 0,
            jnp.broadcast_to(gp[i : i + 1, 0:128], (8, 128)),
            jnp.broadcast_to(gp[i : i + 1, 128:256], (8, 128)),
        )
        for i in range(59)
    ]


def index_rows(idx_ref, raw_ref, order_ref):
    lane = iota((128, 128), 1)
    first = jnp.broadcast_to(idx_ref[:, 0:1], (128, 128))
    second = jnp.broadcast_to(idx_ref[:, 1:2], (128, 128))
    raw_ref[...] = jnp.where(lane == 0, first, second).astype(F32)
    for q in range(8):
        order_ref[q * 16 : (q + 1) * 16, :] = raw_ref[pl.ds((q // 2) * 32 + q % 2, 16, stride=2), :]


def wait_bytes(ref, count, sem):
    block = ref.at[pl.ds(0, count)]
    pltpu.make_async_copy(block, block, sem).wait()


def step_kernel(
    height, columns,
    har_ref, cen_ref, lsc_ref, rot_ref, opa_ref, cam_ref, idx_ref, list_ref, cnt_ref, target_ref,
    rend_ref, depth_ref, gp_ref, grad_ref,
    raw_idx, ord_idx, small, par3, onehot, feat, sq, send1, recv1, send2, recv2, pick, pick_t, expand, fold,
    halo_x, halo_y, raws, trans, weights, dweights, xsplit, acc, image, gimage, fsc,
    back2s, back2r, back1s, back1r, ssem, rsem,
):
    s = lax.axis_index("space")
    y = lax.axis_index("view")
    x = s // 32
    z = (s // 2) % 16
    c = s % 2
    q = x * 2 + c
    up = (s + 127) % 128
    down = (s + 1) % 128

    def place(q2, z2):
        return ((q2 // 2) * 16 + z2) * 2 + q2 % 2

    ring_peers = []
    for e in range(1, 32):
        q2, y2 = (q + e) % 8, (y + e // 8) % 4
        ring_peers.append((y2 * 8 + q2, (place(q2, z), y2)))
    depth_peers = []
    for d in range(1, 16):
        z2 = (z + d) % 16
        depth_peers.append((z2, (place(q, z2), y)))

    barrier = pltpu.get_barrier_semaphore()
    for _, dev in ring_peers + depth_peers + [(0, ((s + 2 * c + 127) % 128, y))]:
        pl.semaphore_signal(barrier, inc=1, device_id=dev, device_id_type=MESH)

    index_rows(idx_ref, raw_idx, ord_idx)
    idx_t = jnp.transpose(ord_idx[...])
    small[...] = jnp.zeros_like(small)
    small[0:3, :] = cen_ref[...]
    small[3:6, :] = lsc_ref[...]
    small[6:10, :] = rot_ref[...]
    small[10:11, :] = opa_ref[...]

    def gather_chunk(i, carry):
        at = pl.ds(pl.multiple_of(i * 256, 256), 256)
        parts = split(jnp.concatenate([har_ref[:, at], small[:, at]], axis=0), 3)
        for n in range(3):
            par3[n * 64 : (n + 1) * 64, at] = parts[n]
        rows = iota((256, 128), 0).astype(F32) + (i * 256).astype(F32)
        onehot[at, 0:128] = one_hot(rows == idx_t[0:1, :])
        onehot[at, 128:256] = one_hot(rows == idx_t[1:2, :])
        return carry

    lax.fori_loop(0, 16, gather_chunk, 0)
    picked = dot(par3[...], onehot[...])
    gp = picked[0:64] + picked[64:128] + picked[128:192]
    gp_ref[...] = gp
    prm = spread_params(gp)
    features = project(
        prm[0:48], prm[48:51], prm[51:54], prm[54:58], prm[58], view_camera(cam_ref), height, columns
    )
    feat[...] = jnp.zeros_like(feat)
    for f in range(10):
        feat[pl.ds(f, 8, stride=16), :] = features[f]
    sq[...] = jnp.transpose(feat[...])
    quarter = iota((8, 128), 1) // 32
    for a in range(4):
        rows = [sq[pl.ds(a * 32 + z4, 8, stride=4), :] for z4 in range(4)]
        for v in range(4):
            out = rows[v]
            for z4 in range(4):
                if z4 != v:
                    out = jnp.where(quarter == z4, pltpu.roll(rows[z4], ((z4 - v) * 32) % 128, axis=1), out)
            send1[v * 8 + 2 * a] = out[0:4]
            send1[v * 8 + 2 * a + 1] = out[4:8]

    pl.semaphore_wait(barrier, 47)

    def send(src, src_at, dst, dst_at, stage, dev):
        pltpu.make_async_remote_copy(
            src_ref=src.at[src_at], dst_ref=dst.at[dst_at], send_sem=ssem.at[stage], recv_sem=rsem.at[stage],
            device_id=dev, device_id_type=MESH,
        ).start()

    me = y * 8 + q
    for at, dev in ring_peers:
        send(send1, at, recv1, me, 0, dev)
    recv1[me] = send1[me]
    for n in range(3):
        send(target_ref, n, halo_y, n, 1, (down, y))
        send(target_ref, n, halo_y, 3 + n, 1, (up, y))

    tl = list_ref[...].astype(F32)
    prow = iota((128, 1), 0)
    label = (((prow % 8) // 2) * 16 + prow // 8) * 4 + (prow % 2) * 2
    for wj in range(8):
        rows = jnp.broadcast_to((label + (wj // 2) * 256 + wj % 2).astype(F32), (128, 128))
        for t in range(8):
            pick[wj * 128 : (wj + 1) * 128, t * 128 : (t + 1) * 128] = one_hot(rows == tl[t : t + 1, :])
    wait_bytes(recv1, 31, rsem.at[0])
    for zq in range(4):
        rows = [recv1[w * 8 : (w + 1) * 8, zq, :] for w in range(4)]
        for z4 in range(4):
            out = rows[z4]
            for w in range(4):
                if w != z4:
                    out = jnp.where(quarter == w, pltpu.roll(rows[w], ((w - z4) * 32) % 128, axis=1), out)
            send2[zq * 4 + z4] = out

    for at, dev in depth_peers:
        send(send2, at, recv2, z, 2, dev)
    recv2[z] = send2[z]

    pcol = iota((1, 128), 1)
    label = (((pcol % 8) // 2) * 16 + pcol // 8) * 4 + (pcol % 2) * 2
    tl_t = jnp.transpose(jnp.concatenate([tl] * 16, axis=0))
    for t in range(8):
        rows = jnp.broadcast_to(tl_t[:, t : t + 1], (128, 128))
        for wj in range(8):
            cols = (label + (wj // 2) * 256 + wj % 2).astype(F32)
            pick_t[t * 128 : (t + 1) * 128, wj * 128 : (wj + 1) * 128] = one_hot(rows == cols)
    row16 = iota((128, 128), 0)
    lane16 = iota((128, 128), 1)
    for f in range(10):
        grow = one_hot(row16 == (lane16 // 16) * 16 + f)
        for n in range(3):
            expand[n * 128 : (n + 1) * 128, f * 128 : (f + 1) * 128] = grow
        if f < 9:
            shrink = one_hot(lane16 == (row16 // 16) * 16 + f)
            for n in range(2):
                fold[f, n * 128 : (n + 1) * 128, :] = shrink
    lower = one_hot(lane16 < row16)
    upper = one_hot(lane16 > row16)
    lower = jnp.concatenate([lower, lower], axis=1)
    upper = jnp.concatenate([upper, upper], axis=1)
    across = jnp.zeros((128, 128), F32)
    down_rows = iota((32, 48), 1) - iota((32, 48), 0) - 3
    down_band = jnp.zeros((32, 48), F32)
    back_rows = iota((16, 32), 0) + 13 - iota((16, 32), 1)
    back_band = jnp.zeros((16, 32), F32)
    for n in range(11):
        across = jnp.where(row16 - lane16 + 5 == n, WINDOW_TAPS[n], across)
        down_band = jnp.where(down_rows == n, WINDOW_TAPS[n], down_band)
        back_band = jnp.where(back_rows == n, WINDOW_TAPS[n], back_band)

    def blur(images):
        tall = dot_exact(down_band, jnp.concatenate(images, axis=1))
        n = len(images)
        flat = jnp.concatenate([tall[:, i * 128 : (i + 1) * 128] for i in range(n)], axis=0)
        flat = dot_exact(flat, across)
        return [flat[i * 32 : (i + 1) * 32] for i in range(n)]

    def with_halo(halo, n, own):
        above = jnp.where(s > 0, halo[n], 0.0)
        below = jnp.where(s < 127, halo[3 + n], 0.0)
        return jnp.concatenate([above, own, below], axis=0)

    wait_bytes(halo_y, 6, rsem.at[1])
    ys = [with_halo(halo_y, n, target_ref[n]) for n in range(3)]
    y_stats = blur(ys + [v * v for v in ys])
    live = jnp.full((128, 128), cnt_ref[0, 7], jnp.int32)
    for t in range(7):
        live = jnp.where(lane16 // 16 == t, cnt_ref[0, t], live)
    live = row16 < live

    wait_bytes(recv2, 15, rsem.at[2])

    rt = jnp.transpose(recv2[...].reshape(128, 128))
    flat = jnp.concatenate([rt[n * 16 : (n + 1) * 16] for n in range(8)], axis=1)
    got = dot(jnp.concatenate(split(flat, 3), axis=0), pick[...])
    got = got[0:16] + got[16:32] + got[32:48]
    stack = jnp.concatenate([got[:, t * 128 : (t + 1) * 128] for t in range(8)], axis=0)
    listed = jnp.transpose(stack)
    wide = dot(jnp.concatenate(split(listed, 3), axis=1), expand[...])
    dx = wide[:, 0:128] - (lane16.astype(F32) + 0.5)
    ca, cb, cc, op = (wide[:, f * 128 : (f + 1) * 128] for f in range(2, 6))
    fsc[0] = wide[:, 128:256]
    fsc[1] = jnp.where(live, -0.5 * ca * dx * dx, -1e30)
    fsc[2] = cb * dx
    fsc[3] = 0.5 * cc
    fsc[4] = op
    for f in range(4):
        fsc[5 + f] = wide[:, (6 + f) * 128 : (7 + f) * 128]
    fsc[9] = ca * dx
    fsc[10] = cb
    fsc[11] = dx
    first_row = (s * TILE).astype(F32) + 0.5

    def alpha_rows(i, carry):
        at = pl.ds(pl.multiple_of(i * 16, 16), 16)
        low = pl.ds(pl.multiple_of(i * 16 + 128, 16), 16)
        r, ax, bx, c2, o = (fsc[n, at, :] for n in range(5))
        for row in range(16):
            dy = r - (first_row + float(row))
            raw = o * jnp.exp(ax - dy * (bx + c2 * dy))
            raws[row, at, :] = raw
            keep = jnp.log(1.0 - jnp.minimum(raw, ALPHA_MAX))
            high, rest = split(keep, 2)
            xsplit[at, row * 128 : (row + 1) * 128] = high
            xsplit[low, row * 128 : (row + 1) * 128] = rest
        return carry

    lax.fori_loop(0, 8, alpha_rows, 0)

    def compose_row(row, carry):
        lanes = pl.ds(pl.multiple_of(row * 128, 128), 128)
        t = jnp.exp(dot(lower, xsplit[:, lanes]))
        w = jnp.minimum(raws[row], ALPHA_MAX) * t
        trans[row] = t
        weights[row] = w
        for f in range(4):
            image[f, pl.ds(row, 1), :] = jnp.sum(w * fsc[5 + f], axis=0, keepdims=True)
        return carry

    lax.fori_loop(0, 16, compose_row, 0)

    for n in range(3):
        send(image, n, halo_x, n, 3, (down, y))
        send(image, n, halo_x, 3 + n, 3, (up, y))
    for n in range(3):
        rend_ref[n] = image[n]
    depth_ref[...] = image[3]
    wait_bytes(halo_x, 6, rsem.at[3])
    xs = [with_halo(halo_x, n, image[n]) for n in range(3)]
    x_stats = blur(xs + [v * v for v in xs] + [xs[n] * ys[n] for n in range(3)])
    grow = s * TILE - 8 + iota((32, 128), 0)
    share = jnp.where((grow >= 0) & (grow < height), -STRUCTURE_WEIGHT / (TILE * TILE), 0.0)
    pulls = []
    for n in range(3):
        mx, exx, exy = x_stats[n], x_stats[3 + n], x_stats[6 + n]
        my, eyy = y_stats[n], y_stats[3 + n]
        a1 = 2.0 * mx * my + STABLE_MEAN
        a2 = 2.0 * (exy - mx * my) + STABLE_SPREAD
        b1 = mx * mx + my * my + STABLE_MEAN
        b2 = (exx - mx * mx) + (eyy - my * my) + STABLE_SPREAD
        inv = share / (b1 * b2)
        ssim = a1 * a2 / (b1 * b2)
        d_exy = 2.0 * a1 * inv
        d_exx = -ssim * b1 * inv
        d_mx = 2.0 * (my * (a2 - a1) * inv - ssim * mx * (b2 - b1) * inv)
        pulls.append((d_mx, d_exx, d_exy))
    nine = [pulls[n][i] for i in range(3) for n in range(3)]
    tall = dot_exact(back_band, jnp.concatenate(nine, axis=1))
    flat = dot_exact(jnp.concatenate([tall[:, i * 128 : (i + 1) * 128] for i in range(9)], axis=0), across)
    for n in range(3):
        vx, vy = image[n], target_ref[n]
        diff = vx - vy
        smooth = (1.0 - STRUCTURE_WEIGHT) / (TILE * TILE) * diff / jnp.sqrt(diff * diff + SMOOTHING**2)
        b_mx, b_xx, b_xy = (flat[(i * 3 + n) * 16 : (i * 3 + n + 1) * 16] for i in range(3))
        gimage[n] = b_mx + 2.0 * vx * b_xx + vy * b_xy + smooth

    def pull_rows(i, carry):
        at = pl.ds(pl.multiple_of(i * 16, 16), 16)
        low = pl.ds(pl.multiple_of(i * 16 + 128, 16), 16)
        colors = [fsc[5 + f, at, :] for f in range(3)]
        for row in range(16):
            dw = sum(gimage[f, row : row + 1, :] * colors[f] for f in range(3))
            dweights[row, at, :] = dw
            high, rest = split(dw * weights[row, at, :], 2)
            xsplit[at, row * 128 : (row + 1) * 128] = high
            xsplit[low, row * 128 : (row + 1) * 128] = rest
        return carry

    lax.fori_loop(0, 8, pull_rows, 0)

    acc[...] = jnp.zeros_like(acc)

    def pull_alpha(row, carry):
        lanes = pl.ds(pl.multiple_of(row * 128, 128), 128)
        later = dot(upper, xsplit[:, lanes])
        raw = raws[row]
        d_alpha = dweights[row] * trans[row] - later / (1.0 - jnp.minimum(raw, ALPHA_MAX))
        d_power = d_alpha * jnp.where(raw < ALPHA_MAX, raw, jnp.where(raw == ALPHA_MAX, 0.5 * raw, 0.0))
        dy = fsc[0] - (first_row + row.astype(F32))
        moved = d_power * dy
        acc[0] += d_power
        acc[1] += moved
        acc[2] += moved * dy
        w = weights[row]
        for f in range(3):
            acc[3 + f] += w * gimage[f, pl.ds(row, 1), :]
        return carry

    lax.fori_loop(0, 16, pull_alpha, 0)
    s0, s1, s2 = acc[0], acc[1], acc[2]
    adx, cb, dx = fsc[9], fsc[10], fsc[11]
    grads = [
        -(adx * s0 + cb * s1),
        -(2.0 * fsc[3] * s1 + fsc[2] * s0),
        -0.5 * dx * dx * s0,
        -dx * s1,
        -0.5 * s2,
        s0 / fsc[4],
        acc[3],
        acc[4],
        acc[5],
    ]
    folded = sum(dot(jnp.concatenate(split(grads[f], 2), axis=1), fold[f]) for f in range(9))
    turned = jnp.transpose(folded)
    flat = jnp.concatenate([turned[t * 16 : (t + 1) * 16] for t in range(8)], axis=1)
    put = dot(jnp.concatenate(split(flat, 3), axis=0), pick_t[...])
    put = put[0:16] + put[16:32] + put[32:48]
    stack = jnp.concatenate([put[:, n * 128 : (n + 1) * 128] for n in range(8)], axis=0)
    back2s[...] = jnp.transpose(stack).reshape(16, 8, 128)

    for at, dev in depth_peers:
        send(back2s, at, back2r, z, 4, dev)
    back2r[z] = back2s[z]
    wait_bytes(back2r, 15, rsem.at[4])
    for zq in range(4):
        for w in range(4):
            out = back2r[zq * 4 + w]
            for z4 in range(4):
                if z4 != w:
                    moved = pltpu.roll(back2r[zq * 4 + z4], ((z4 - w) * 32) % 128, axis=1)
                    out = jnp.where(quarter == z4, moved, out)
            back1s[w * 8 : (w + 1) * 8, zq, :] = out
    for at, dev in ring_peers:
        send(back1s, at, back1r, me, 5, dev)
    back1r[me] = back1s[me]
    wait_bytes(back1r, 31, rsem.at[5])
    for a in range(4):
        rows = [
            jnp.concatenate([back1r[v * 8 + 2 * a], back1r[v * 8 + 2 * a + 1]], axis=0) for v in range(4)
        ]
        for z4 in range(4):
            out = rows[z4]
            for v in range(4):
                if v != z4:
                    out = jnp.where(quarter == v, pltpu.roll(rows[v], ((v - z4) * 32) % 128, axis=1), out)
            sq[pl.ds(a * 32 + z4, 8, stride=4), :] = out
    grad_ref[...] = jnp.transpose(sq[...])

    wait_bytes(send1, 31, ssem.at[0])
    wait_bytes(halo_y, 6, ssem.at[1])
    wait_bytes(send2, 15, ssem.at[2])
    wait_bytes(halo_x, 6, ssem.at[3])
    wait_bytes(back2s, 15, ssem.at[4])
    wait_bytes(back1s, 31, ssem.at[5])


def owner_kernel(
    height, columns,
    grad_ref, gp_ref, cam_ref, idx_ref,
    har_ref, cen_ref, lsc_ref, rot_ref, opa_ref,
    raw_idx, ord_idx, rows_ref,
):
    prm = spread_params(gp_ref[...])
    cotangents = [grad_ref[pl.ds(f, 8, stride=16), :] for f in range(9)]
    cotangents.append(jnp.zeros((8, 128), F32))
    camera = view_camera(cam_ref)

    def run(harmonics, center, log_scale, quaternion, opacity):
        return project(harmonics, center, log_scale, quaternion, opacity, camera, height, columns)

    _, pull = jax.vjp(run, prm[0:48], prm[48:51], prm[51:54], prm[54:58], prm[58])
    d_har, d_cen, d_lsc, d_rot, d_opa = pull(cotangents)
    rows = list(d_har) + list(d_cen) + list(d_lsc) + list(d_rot) + [d_opa]
    for i in range(59):
        rows_ref[i * 8 : (i + 1) * 8, :] = rows[i]
    for i in range(59, 64):
        rows_ref[i * 8 : (i + 1) * 8, :] = jnp.zeros((8, 128), F32)
    halves = [sum(rows_ref[pl.ds(v * 2 + j, 64, stride=8), :] for v in range(4)) for j in range(2)]
    lhs = jnp.concatenate(split(jnp.concatenate(halves, axis=1), 2), axis=0)
    index_rows(idx_ref, raw_idx, ord_idx)
    first = jnp.broadcast_to(ord_idx[:, 0:1], (128, 256))
    second = jnp.broadcast_to(ord_idx[:, 1:2], (128, 256))

    def put_chunk(i, carry):
        at = pl.ds(pl.multiple_of(i * 256, 256), 256)
        cols = iota((128, 256), 1).astype(F32) + (i * 256).astype(F32)
        hot = jnp.concatenate([one_hot(first == cols), one_hot(second == cols)], axis=0)
        out = dot(lhs, hot)
        out = out[0:64] + out[64:128]
        har_ref[:, at] = out[0:48]
        cen_ref[:, at] = out[48:51]
        lsc_ref[:, at] = out[51:54]
        rot_ref[:, at] = out[54:58]
        opa_ref[:, at] = out[58:59]
        return carry

    lax.fori_loop(0, 16, put_chunk, 0)


def on_device(
    centers, log_scales, rotations, opacity, harmonics, cameras, send_index, tile_lists, counts, target
):
    strips = lax.axis_size("space")
    height = TILE * strips
    columns = target.shape[-1]
    count = centers.shape[1]
    vmem = pl.BlockSpec(memory_space=VMEM)
    smem = pl.BlockSpec(memory_space=pltpu.SMEM)
    index = send_index.reshape(strips, 2)
    dma = pltpu.SemaphoreType.DMA

    def shape(*dims):
        return jax.ShapeDtypeStruct(dims, F32)

    rendered, inverse_depth, gathered, grads = pl.pallas_call(
        functools.partial(step_kernel, height, columns),
        out_shape=[shape(3, 16, 128), shape(16, 128), shape(64, 256), shape(128, 128)],
        in_specs=[vmem] * 5 + [smem, vmem, vmem, smem, vmem],
        out_specs=[vmem] * 4,
        scratch_shapes=[
            VMEM((128, 128), F32),
            VMEM((128, 128), F32),
            VMEM((16, count), F32),
            VMEM((192, count), BF16),
            VMEM((count, 256), BF16),
            VMEM((128, 128), F32),
            VMEM((128, 128), F32),
            VMEM((32, 4, 128), F32),
            VMEM((32, 4, 128), F32),
            VMEM((16, 8, 128), F32),
            VMEM((16, 8, 128), F32),
            VMEM((1024, 1024), BF16),
            VMEM((1024, 1024), BF16),
            VMEM((384, 1280), BF16),
            VMEM((9, 256, 128), BF16),
            VMEM((6, 16, 128), F32),
            VMEM((6, 16, 128), F32),
            VMEM((16, 128, 128), F32),
            VMEM((16, 128, 128), F32),
            VMEM((16, 128, 128), F32),
            VMEM((16, 128, 128), F32),
            VMEM((256, 2048), BF16),
            VMEM((6, 128, 128), F32),
            VMEM((4, 16, 128), F32),
            VMEM((3, 16, 128), F32),
            VMEM((12, 128, 128), F32),
            VMEM((16, 8, 128), F32),
            VMEM((16, 8, 128), F32),
            VMEM((32, 4, 128), F32),
            VMEM((32, 4, 128), F32),
            dma((6,)),
            dma((6,)),
        ],
        compiler_params=pltpu.CompilerParams(
            collective_id=0, has_side_effects=True, vmem_limit_bytes=48 * 2**20
        ),
        name="render_step",
    )(
        harmonics.reshape(48, count),
        centers,
        log_scales,
        rotations,
        opacity.reshape(1, count),
        cameras,
        index,
        tile_lists[0],
        counts,
        target[0],
    )
    d_har, d_cen, d_lsc, d_rot, d_opa = pl.pallas_call(
        functools.partial(owner_kernel, height, columns),
        out_shape=[shape(48, count), shape(3, count), shape(3, count), shape(4, count), shape(1, count)],
        in_specs=[vmem, vmem, smem, vmem],
        out_specs=[vmem] * 5,
        scratch_shapes=[VMEM((128, 128), F32), VMEM((128, 128), F32), VMEM((512, 128), F32)],
        compiler_params=pltpu.CompilerParams(vmem_limit_bytes=32 * 2**20),
        name="owner_pull",
    )(grads, gathered, cameras, index)
    return (
        rendered[None],
        inverse_depth[None],
        d_cen,
        d_lsc,
        d_rot,
        d_opa.reshape(count),
        d_har.reshape(3, 16, count),
    )


def solution(mesh):
    return jax.shard_map(
        on_device,
        mesh=mesh,
        in_specs=(
            P(None, ("space", "view")),
            P(None, ("space", "view")),
            P(None, ("space", "view")),
            P(("space", "view")),
            P(None, None, ("space", "view")),
            P(),
            P("space", "view", None, None),
            P("space", None, None),
            P("space", None),
            P("view", None, "space", None),
        ),
        out_specs=(
            P("view", None, "space", None),
            P("view", "space", None),
            P(None, ("space", "view")),
            P(None, ("space", "view")),
            P(None, ("space", "view")),
            P(("space", "view")),
            P(None, None, ("space", "view")),
        ),
        check_vma=False,
    )
```

time: 241 us -> 70.1 us (0.29); the launches traced: 238 us -> 69.6 us
  Pallas kernels: 0 us -> 62 us
  other arithmetic: 51.1 us -> 0 us
  waiting for transfers between devices: 46.4 us -> 0 us
  blocking collectives: 42.9 us -> 0 us
  starting transfers between devices: 40.5 us -> 0 us
  local copies, waits for them, and re-layouts: 44.5 us -> 6.92 us
  matrix products: 10.8 us -> 0 us
    pallas_call x0 -> x2, Pallas kernels: none -> 62 us  [the longest x1 57.4 us: on_device(): pl.pallas_call(functools.partial(step_kernel, height, columns), out_shape...]
    all_to_all x1 -> x0, blocking collectives: 42.9 us -> none  [on_device(): lax.all_to_all(backward, 'space', split_axis=2, concat_axis=2, tiled=True)]
    all_to_all x3 -> x0, waiting for transfers between devices: 40.7 us -> none  [the longest x1 33 us: on_device(): lax.all_to_all(outgoing, 'space', split_axis=2, concat_axis=2, tiled=True)]
    scatter-add x2 -> x0, other arithmetic: 31.6 us -> none  [the longest x1 25 us: owner_project(): features = jnp.take(everyone, chosen, axis=-1)]
    all_to_all x3 -> x0, starting transfers between devices: 28.1 us -> none  [the longest x1 20.4 us: on_device(): lax.all_to_all(outgoing, 'space', split_axis=2, concat_axis=2, tiled=True)]
    ppermute x4 -> x0, starting transfers between devices: 12.5 us -> none  [the longest x2 8.15 us: extended(): lax.ppermute(lax.slice_in_dim(block, block.shape[dim] - width, None, axis...]
    dot_general x6 -> x0, matrix products: 10.8 us -> none  [the longest x3 6.63 us: composite_block(): jnp.einsum('tpk,kl->tpl', log_keep, upper_ones, precision=lax.Precision.H...]
    gather x4 -> x0, local copies, waits for them, and re-layouts: 7.59 us -> none  [the longest x2 4.59 us: owner_project(): features = jnp.take(everyone, chosen, axis=-1)]
  transfers between devices with their start and end apart: 7 -> 0, of which waited for: 5 -> 0; matrix products, arithmetic and copies ran while one was open for 0% -> 0% of each run, Pallas kernels for 0% -> 0%
where the time goes in v1:
time: 70.1 us; the launch traced here: 69.6 us
  Pallas kernels  62 us (88%)
  local copies, waits for them, and re-layouts  6.92 us (10%)
    pallas_call x1, Pallas kernels, on_device(): pl.pallas_call(functools.partial(step_kernel, height, columns), out_shape...  57.4 us
    unnamed x21, local copies, waits for them, and re-layouts  6.92 us
    pallas_call x1, Pallas kernels, on_device(): pl.pallas_call(functools.partial(owner_kernel, height, columns), out_shap...  4.63 us

profile of v1, /device:TPU:1, one launch (start us, length us, event | category | flops | bytes accessed | tf_op | source)
XLA Modules:
  0.0 69.6 jit_solution(12583235605675890014)
XLA Ops:
  0.6 0.0 copy-start.1
  0.6 0.0 copy-start.6
  0.7 0.0 copy-start.7
  0.7 0.8 %copy.17 = s32[1,1,128,2]{3,2,1,0:T(8,128)S(1)} copy(s32[1,1,128,2]{2,3,1,0:T(2,128)} %param.16) | data formatting | bytes 2048 | tf_op args[6]
  1.5 0.0 copy-start.8
  1.5 0.0 copy-done.1
  1.5 0.0 copy-done.6
  1.5 0.0 copy-done.7
  1.5 0.6 copy-done.8
  2.1 0.0 copy-start
  2.1 1.1 %copy-done = f32[3,16,4096]{2,1,0:T(8,128)S(1)} copy-done((f32[3,16,4096]{2,1,0:T(8,128)S(1)}, f32[3,16,4096]{2,1,0:T(8,128)}, u32[]{:S(2)}) %copy-start) | copy-done | bytes 786456
  3.3 0.0 copy-start.2
  3.3 0.8 %copy-done.2 = f32[3,4096]{1,0:T(4,128)S(1)} copy-done((f32[3,4096]{1,0:T(4,128)S(1)}, f32[3,4096]{1,0:T(4,128)}, u32[]{:S(2)}) %copy-start.2) | copy-done | bytes 49176
  4.1 0.0 copy-start.3
  4.1 0.8 %copy-done.3 = f32[4,4096]{1,0:T(4,128)S(1)} copy-done((f32[4,4096]{1,0:T(4,128)S(1)}, f32[4,4096]{1,0:T(4,128)}, u32[]{:S(2)}) %copy-start.3) | copy-done | bytes 65560
  5.0 0.0 copy-start.4
  5.0 0.7 %copy-done.4 = f32[1,3,16,128]{3,2,1,0:T(8,128)S(1)} copy-done((f32[1,3,16,128]{3,2,1,0:T(8,128)S(1)}, f32[1,3,16,128]{3,2,1,0:T(8,128)}, u32[]{:S(2)}) %copy-start.4) | copy-done | bytes 24600
  5.7 0.0 copy-start.5
  5.7 0.7 %copy-done.5 = f32[4096]{0:T(1024)S(1)} copy-done((f32[4096]{0:T(1024)S(1)}, f32[4096]{0:T(1024)}, u32[]{:S(2)}) %copy-start.5) | copy-done | bytes 16408
  6.4 57.4 %render_step.1 = (f32[3,16,128]{2,1,0:T(8,128)S(1)}, f32[16,128]{1,0:T(8,128)S(1)}, f32[64,256]{1,0:T(8,128)S(1)}, f32[128,128]{1,0:T(8,128)S(1)}) custom-call(f32[48,4096]{1,0:T(8,128)S(1)} %bitcast.9, f32[3,4096]{1,0:T(4,128)S(1)} %copy-done.1, f32[3,4096]{1,0:T(4,128)S(1)} %copy-done.2, f32[4,4096]{1,0:T(4,128)S(1)} %copy-done.3, f32[1,4096]{1,0:T(1,128)S(1)} %bitcast.14, ...), custom_call_target="tpu_custom_call" | custom-call | tf_op jit(solution)/shard_map/render_step/pallas_call | solution.py:567
  63.8 4.6 %owner_pull.1 = (f32[48,4096]{1,0:T(8,128)}, f32[3,4096]{1,0:T(4,128)}, f32[3,4096]{1,0:T(4,128)}, f32[4,4096]{1,0:T(4,128)}, f32[1,4096]{1,0:T(1,128)}) custom-call(f32[128,128]{1,0:T(8,128)S(1)} %get-tuple-element.18.grad_ref, f32[64,256]{1,0:T(8,128)S(1)} %get-tuple-element.19.gp_ref, f32[4,3]{1,0:T(4,128)S(1)} %copy-done.6, s32[128,2]{1,0:T(8,128)S(1)} %bitcast.11), custom_call_target="tpu_custom_call" | custom-call | tf_op jit(solution)/shard_map/owner_pull/pallas_call | solution.py:622
  68.4 0.6 copy.20
  69.0 0.6 copy.21
Async XLA Ops:
  0.6 0.9 %copy-start.1 = (f32[3,4096]{1,0:T(4,128)S(1)}, f32[3,4096]{1,0:T(4,128)}, u32[]{:S(2)}) copy-start(f32[3,4096]{1,0:T(4,128)} %cen_ref.1) | copy-start | bytes 147460
  0.6 0.9 %copy-start.6 = (f32[4,3]{1,0:T(4,128)S(1)}, f32[4,3]{1,0:T(4,128)}, u32[]{:S(2)}) copy-start(f32[4,3]{1,0:T(4,128)} %cam_ref.3) | copy-start | bytes 148
  0.7 0.9 %copy-start.7 = (s32[1,8,128]{2,1,0:T(8,128)S(1)}, s32[1,8,128]{2,1,0:T(8,128)}, u32[]{:S(2)}) copy-start(s32[1,8,128]{2,1,0:T(8,128)} %param.17) | copy-start | bytes 12292
  1.5 0.7 copy-start.8
  2.1 1.1 %copy-start = (f32[3,16,4096]{2,1,0:T(8,128)S(1)}, f32[3,16,4096]{2,1,0:T(8,128)}, u32[]{:S(2)}) copy-start(f32[3,16,4096]{2,1,0:T(8,128)} %param.14) | copy-start | bytes 2359300
  3.3 0.8 %copy-start.2 = (f32[3,4096]{1,0:T(4,128)S(1)}, f32[3,4096]{1,0:T(4,128)}, u32[]{:S(2)}) copy-start(f32[3,4096]{1,0:T(4,128)} %lsc_ref.1) | copy-start | bytes 147460
  4.1 0.8 %copy-start.3 = (f32[4,4096]{1,0:T(4,128)S(1)}, f32[4,4096]{1,0:T(4,128)}, u32[]{:S(2)}) copy-start(f32[4,4096]{1,0:T(4,128)} %rot_ref.1) | copy-start | bytes 196612
  5.0 0.7 %copy-start.4 = (f32[1,3,16,128]{3,2,1,0:T(8,128)S(1)}, f32[1,3,16,128]{3,2,1,0:T(8,128)}, u32[]{:S(2)}) copy-start(f32[1,3,16,128]{3,2,1,0:T(8,128)} %param.19) | copy-start | bytes 73732
  5.7 0.7 %copy-start.5 = (f32[4096]{0:T(1024)S(1)}, f32[4096]{0:T(1024)}, u32[]{:S(2)}) copy-start(f32[4096]{0:T(1024)} %param.13) | copy-start | bytes 49156

commit v2 on v1

v2 whole, which is shorter than its diff:
```python
import functools
import math

import jax
import jax.numpy as jnp
from jax import lax
from jax.experimental import pallas as pl
from jax.experimental.pallas import tpu as pltpu
from jax.sharding import PartitionSpec as P

TILE = 16
FOCAL_LENGTH = 512.0
LOW_PASS = 0.3
ALPHA_MAX = 0.99
SMOOTHING = 0.05
STRUCTURE_WEIGHT = 0.2
STABLE_MEAN = 0.0001
STABLE_SPREAD = 0.0009
HARMONIC_ZERO = 0.28209479177387814
HARMONIC_ONE = 0.4886025119029199
HARMONIC_TWO = [
    1.0925484305920792,
    -1.0925484305920792,
    0.31539156525252005,
    -1.0925484305920792,
    0.5462742152960396,
]
HARMONIC_THREE = [
    -0.5900435899266435,
    2.890611442640554,
    -0.4570457994644658,
    0.3731763325901154,
    -0.4570457994644658,
    1.445305721320277,
    -0.5900435899266435,
]
TAPS_RAW = [math.exp(-((offset - 5) ** 2) / 4.5) for offset in range(11)]
WINDOW_TAPS = [value / sum(TAPS_RAW) for value in TAPS_RAW]

F32 = jnp.float32
BF16 = jnp.bfloat16
MESH = pl.DeviceIdType.MESH
VMEM = pltpu.VMEM
EXACT = lax.Precision.HIGHEST


def harmonic_basis(ux, uy, uz):
    xx, yy, zz = ux * ux, uy * uy, uz * uz
    return [
        HARMONIC_ZERO * jnp.ones_like(ux),
        -HARMONIC_ONE * uy,
        HARMONIC_ONE * uz,
        -HARMONIC_ONE * ux,
        HARMONIC_TWO[0] * ux * uy,
        HARMONIC_TWO[1] * uy * uz,
        HARMONIC_TWO[2] * (2.0 * zz - xx - yy),
        HARMONIC_TWO[3] * ux * uz,
        HARMONIC_TWO[4] * (xx - yy),
        HARMONIC_THREE[0] * uy * (3.0 * xx - yy),
        HARMONIC_THREE[1] * ux * uy * uz,
        HARMONIC_THREE[2] * uy * (4.0 * zz - xx - yy),
        HARMONIC_THREE[3] * uz * (2.0 * zz - 3.0 * xx - 3.0 * yy),
        HARMONIC_THREE[4] * ux * (4.0 * zz - xx - yy),
        HARMONIC_THREE[5] * uz * (xx - yy),
        HARMONIC_THREE[6] * ux * (xx - 3.0 * yy),
    ]


def geometry(center, log_scale, quaternion, camera, height, columns):
    tx, ty, tz = (center[i] - camera[i] for i in range(3))
    iz = 1.0 / tz
    u = FOCAL_LENGTH * tx * iz + 0.5 * columns
    r = FOCAL_LENGTH * ty * iz + 0.5 * height
    qw, qx, qy, qz = quaternion
    s = 2.0 / (qw * qw + qx * qx + qy * qy + qz * qz)
    rot = [
        [1.0 - s * (qy * qy + qz * qz), s * (qx * qy - qw * qz), s * (qx * qz + qw * qy)],
        [s * (qx * qy + qw * qz), 1.0 - s * (qx * qx + qz * qz), s * (qy * qz - qw * qx)],
        [s * (qx * qz - qw * qy), s * (qy * qz + qw * qx), 1.0 - s * (qx * qx + qy * qy)],
    ]
    scales = [jnp.exp(v) for v in log_scale]
    m = [[rot[i][j] * scales[j] for j in range(3)] for i in range(3)]

    def entry(i, j):
        return m[i][0] * m[j][0] + m[i][1] * m[j][1] + m[i][2] * m[j][2]

    ja = FOCAL_LENGTH * iz
    jx = -FOCAL_LENGTH * tx * iz * iz
    jy = -FOCAL_LENGTH * ty * iz * iz
    sxz, syz, szz = entry(0, 2), entry(1, 2), entry(2, 2)
    pa = ja * ja * entry(0, 0) + 2.0 * ja * jx * sxz + jx * jx * szz + LOW_PASS
    pb = ja * ja * entry(0, 1) + ja * jy * sxz + jx * ja * syz + jx * jy * szz
    pc = ja * ja * entry(1, 1) + 2.0 * ja * jy * syz + jy * jy * szz + LOW_PASS
    det = pa * pc - pb * pb
    return u, r, pc / det, -pb / det, pa / det, iz


def directions(center, camera):
    tx, ty, tz = (center[i] - camera[i] for i in range(3))
    length = jnp.sqrt(tx * tx + ty * ty + tz * tz)
    return harmonic_basis(tx / length, ty / length, tz / length)


def raw_color(harmonics, basis, channel):
    total = harmonics[channel * 16] * basis[0]
    for i in range(1, 16):
        total = total + harmonics[channel * 16 + i] * basis[i]
    return 0.5 + total


def iota(shape, dim):
    return lax.broadcasted_iota(jnp.int32, shape, dim)


def one_hot(condition):
    return jnp.where(condition, 1.0, 0.0).astype(BF16)


def split(value, parts):
    out = []
    for _ in range(parts - 1):
        high = value.astype(BF16)
        out.append(high)
        value = value - high.astype(F32)
    out.append(value.astype(BF16))
    return out


def dot(a, b):
    return jnp.dot(a, b, preferred_element_type=F32)


def dot_exact(a, b):
    return jnp.dot(a, b, preferred_element_type=F32, precision=EXACT)


def take_lanes(values, lanes):
    return jnp.take_along_axis(values, lanes, axis=1, mode="promise_in_bounds")


def view_camera(cam_ref):
    view = iota((8, 128), 0) // 2
    out = []
    for i in range(3):
        value = jnp.broadcast_to(cam_ref[3:4, i : i + 1], (8, 128))
        for v in range(3):
            value = jnp.where(view == v, cam_ref[v : v + 1, i : i + 1], value)
        out.append(value)
    return out


def spread_params(first, second):
    even = iota((8, 128), 0) % 2 == 0
    return [
        jnp.where(
            even,
            jnp.broadcast_to(first[i : i + 1], (8, 128)),
            jnp.broadcast_to(second[i : i + 1], (8, 128)),
        )
        for i in range(59)
    ]


def wait_bytes(ref, count, sem):
    block = ref.at[pl.ds(0, count)]
    pltpu.make_async_copy(block, block, sem).wait()


def step_kernel(
    height, columns,
    har_hbm, cen_hbm, lsc_hbm, rot_hbm, opa_hbm, cam_hbm, idx_hbm, list_hbm, cnt_hbm, target_hbm,
    rend_hbm, depth_hbm, jac_hbm, inv_hbm, grad_hbm,
    har_ref, cen_ref, lsc_ref, rot_ref, opa_ref, cam_ref, idx_ref, list_ref, cnt_ref, target_ref,
    small, feat, sq, send1, recv1, send2, recv2, fold,
    halo_x, halo_y, raws, trans, weights, dweights, xsplit, acc, image, gimage, fsc,
    back2s, back2r, back1s, back1r, jac_ref, inv_ref, lsem, ssem, rsem,
):
    s = lax.axis_index("space")
    y = lax.axis_index("view")
    x = s // 32
    z = (s // 2) % 16
    c = s % 2
    q = x * 2 + c
    up = (s + 127) % 128
    down = (s + 1) % 128

    quarter = iota((8, 128), 1) // 32

    def place(q2, z2):
        return ((q2 // 2) * 16 + z2) * 2 + q2 % 2

    ring_peers = []
    for e in range(1, 32):
        q2, y2 = (q + e) % 8, (y + e // 8) % 4
        ring_peers.append((y2 * 8 + q2, (place(q2, z), y2)))
    depth_peers = []
    for d in (8, 7, 9, 6, 10, 5, 11, 4, 12, 3, 13, 2, 14, 1, 15):
        z2 = (z + d) % 16
        depth_peers.append((z2, (place(q, z2), y)))

    barrier = pltpu.get_barrier_semaphore()
    for _, dev in depth_peers + ring_peers + [(0, ((s + 2 * c + 127) % 128, y))]:
        pl.semaphore_signal(barrier, inc=1, device_id=dev, device_id_type=MESH)
    loads = [
        pltpu.make_async_copy(source, place_in, lsem.at[n])
        for n, (source, place_in) in enumerate((
            (idx_hbm, idx_ref), (har_hbm, har_ref), (cen_hbm, cen_ref), (lsc_hbm, lsc_ref), (rot_hbm, rot_ref),
            (opa_hbm, opa_ref), (cam_hbm, cam_ref), (list_hbm, list_ref), (cnt_hbm, cnt_ref), (target_hbm, target_ref),
        ))
    ]
    for load in loads:
        load.start()
    for load in loads:
        load.wait()

    small[...] = jnp.zeros_like(small)
    small[0:3, :] = cen_ref[...]
    small[3:6, :] = lsc_ref[...]
    small[6:10, :] = rot_ref[...]
    small[10:11, :] = opa_ref[...]
    number = idx_ref[...]
    chunk_of = [jnp.broadcast_to(number[j : j + 1] // 128, (64, 128)) for j in range(2)]
    lane_of = [jnp.broadcast_to(number[j : j + 1] % 128, (64, 128)) for j in range(2)]

    def gather_chunk(i, carry):
        at = pl.ds(pl.multiple_of(i * 128, 128), 128)
        block = jnp.concatenate([har_ref[:, at], small[:, at]], axis=0)
        return tuple(jnp.where(chunk_of[j] == i, take_lanes(block, lane_of[j]), carry[j]) for j in range(2))

    zero = jnp.zeros((64, 128), F32)
    picked = lax.fori_loop(0, har_ref.shape[1] // 128, gather_chunk, (zero, zero), unroll=4)
    prm = spread_params(*picked)
    camera = view_camera(cam_ref)
    center, log_scale, quaternion = prm[48:51], prm[51:54], prm[54:58]
    u, r, ca, cb, cc, iz = geometry(center, log_scale, quaternion, camera, height, columns)
    opaque = 1.0 / (1.0 + jnp.exp(-prm[58]))
    basis = directions(center, camera)
    raw_colors = [raw_color(prm, basis, ch) for ch in range(3)]
    features = [u, r, ca, cb, cc, opaque] + [jnp.maximum(0.0, v) for v in raw_colors] + [iz]
    feat[...] = jnp.zeros_like(feat)
    for f in range(10):
        feat[pl.ds(f, 8, stride=16), :] = features[f]
    sq[...] = jnp.transpose(feat[...])
    for a in range(8):
        first = (a // 2) * 32 + a % 2
        rows = [sq[pl.ds(first + z4 * 2, 4, stride=8), :] for z4 in range(4)]
        for v in range(4):
            out = rows[v]
            for z4 in range(4):
                if z4 != v:
                    moved = pltpu.roll(rows[z4], ((z4 - v) * 32) % 128, axis=1)
                    out = jnp.where(quarter[0:4] == z4, moved, out)
            send1[v * 8 + a] = out

    pl.semaphore_wait(barrier, 47)

    def send(src, src_at, dst, dst_at, stage, dev):
        pltpu.make_async_remote_copy(
            src_ref=src.at[src_at], dst_ref=dst.at[dst_at], send_sem=ssem.at[stage], recv_sem=rsem.at[stage],
            device_id=dev, device_id_type=MESH,
        ).start()

    me = y * 8 + q
    for at, dev in ring_peers:
        send(send1, at, recv1, me, 0, dev)
    recv1[me] = send1[me]
    for n in range(3):
        send(target_ref, n, halo_y, n, 1, (down, y))
        send(target_ref, n, halo_y, 3 + n, 1, (up, y))

    _, pull = jax.vjp(
        lambda *a: geometry(*a, camera, height, columns)[2:5], center, log_scale, quaternion
    )
    one, none = jnp.ones((8, 128), F32), jnp.zeros((8, 128), F32)
    jac = []
    for i in range(3):
        d_center, d_scale, d_turn = pull(tuple(one if i == n else none for n in range(3)))
        jac += list(d_center) + list(d_scale) + list(d_turn)
    passed = [jnp.where(v > 0.0, 1.0, jnp.where(v == 0.0, 0.5, 0.0)) for v in raw_colors]
    for ch in range(3):
        _, pull = jax.vjp(lambda a: raw_color(prm, directions(a, camera), ch), center)
        jac += [passed[ch] * v for v in pull(one)[0]]
    shift = [center[i] - camera[i] for i in range(2)]
    jac += [FOCAL_LENGTH * iz] + [-FOCAL_LENGTH * v * iz * iz for v in shift]
    jac += [opaque * (1.0 - opaque)] + passed + basis
    for n, value in enumerate(jac):
        jac_ref[n] = value

    row128 = iota((128, 128), 0)
    lane128 = iota((128, 128), 1)
    columns_of = jnp.transpose(jnp.concatenate([number.astype(F32)] * 64, axis=0)).astype(jnp.int32)
    total = jnp.zeros((32, 128), F32)
    for j in range(2):
        hit = chunk_of[j][0:32] == iota((32, 128), 0)
        value = jnp.where(hit, (iota((32, 128), 1) + (1 + j * 128)).astype(F32), 0.0).astype(BF16)
        total = total + dot(value, one_hot(columns_of[:, j : j + 1] % 128 == lane128))
    inv_ref[...] = total.astype(jnp.int32)
    stores = [
        pltpu.make_async_copy(jac_ref, jac_hbm, lsem.at[10]),
        pltpu.make_async_copy(inv_ref, inv_hbm, lsem.at[11]),
        pltpu.make_async_copy(image.at[pl.ds(0, 3)], rend_hbm, lsem.at[12]),
        pltpu.make_async_copy(image.at[3], depth_hbm, lsem.at[13]),
        pltpu.make_async_copy(sq, grad_hbm, lsem.at[14]),
    ]
    stores[0].start()
    stores[1].start()

    slot = list_ref[...]
    block_of = (slot // 256) * 2 + slot % 2
    source = (slot // 2) % 128
    lane_in = ((source // 2) % 16) * 8 + (source // 32) * 2 + source % 2
    lane_cols = jnp.transpose(jnp.concatenate([lane_in.astype(F32)] * 16, axis=0)).astype(jnp.int32)
    inverse = jnp.zeros((16, 128), F32)
    for t in range(8):
        hit = jnp.broadcast_to(block_of[t : t + 1], (8, 128)) == iota((8, 128), 0)
        value = jnp.concatenate(
            [jnp.where(hit, float(t), 0.0), jnp.where(hit, iota((8, 128), 1).astype(F32), 0.0)], axis=0
        ).astype(BF16)
        inverse = inverse + dot(value, one_hot(lane_cols[:, t : t + 1] == lane128))
    inverse = inverse.astype(jnp.int32)
    tile_from, entry_from = inverse[0:8], inverse[8:16]
    wait_bytes(recv1, 31, rsem.at[0])
    for zq in range(4):
        rows = [recv1[w * 8 : (w + 1) * 8, zq, :] for w in range(4)]
        for z4 in range(4):
            out = rows[z4]
            for w in range(4):
                if w != z4:
                    out = jnp.where(quarter == w, pltpu.roll(rows[w], ((w - z4) * 32) % 128, axis=1), out)
            send2[zq * 4 + z4] = out

    for at, dev in depth_peers:
        send(send2, at, recv2, z, 2, dev)
    recv2[z] = send2[z]

    row16, lane16 = row128, lane128
    for f in range(9):
        shrink = one_hot(lane16 == (row16 // 16) * 16 + f)
        for n in range(2):
            fold[f, n * 128 : (n + 1) * 128, :] = shrink
    lower = one_hot(lane16 < row16)
    upper = one_hot(lane16 > row16)
    lower = jnp.concatenate([lower, lower], axis=1)
    upper = jnp.concatenate([upper, upper], axis=1)
    across = jnp.zeros((128, 128), F32)
    down_rows = iota((32, 48), 1) - iota((32, 48), 0) - 3
    down_band = jnp.zeros((32, 48), F32)
    back_rows = iota((16, 32), 0) + 13 - iota((16, 32), 1)
    back_band = jnp.zeros((16, 32), F32)
    for n in range(11):
        across = jnp.where(row16 - lane16 + 5 == n, WINDOW_TAPS[n], across)
        down_band = jnp.where(down_rows == n, WINDOW_TAPS[n], down_band)
        back_band = jnp.where(back_rows == n, WINDOW_TAPS[n], back_band)

    def blur(images):
        tall = dot_exact(down_band, jnp.concatenate(images, axis=1))
        n = len(images)
        flat = jnp.concatenate([tall[:, i * 128 : (i + 1) * 128] for i in range(n)], axis=0)
        flat = dot_exact(flat, across)
        return [flat[i * 32 : (i + 1) * 32] for i in range(n)]

    def with_halo(halo, n, own):
        above = jnp.where(s > 0, halo[n], 0.0)
        below = jnp.where(s < 127, halo[3 + n], 0.0)
        return jnp.concatenate([above, own, below], axis=0)

    wait_bytes(halo_y, 6, rsem.at[1])
    ys = [with_halo(halo_y, n, target_ref[n]) for n in range(3)]
    y_stats = blur(ys + [v * v for v in ys])
    live = jnp.broadcast_to(cnt_ref[:, 7:8], (128, 128))
    for t in range(7):
        live = jnp.where(lane16 // 16 == t, cnt_ref[:, t : t + 1], live)
    live = row16 < live

    wait_bytes(recv2, 15, rsem.at[2])

    rt = jnp.transpose(recv2[...].reshape(128, 128))
    tiles = []
    for t in range(8):
        block = jnp.broadcast_to(block_of[t : t + 1], (16, 128))
        lanes = jnp.broadcast_to(lane_in[t : t + 1], (16, 128))
        got = take_lanes(rt[0:16], lanes)
        for n in range(1, 8):
            got = jnp.where(block == n, take_lanes(rt[n * 16 : (n + 1) * 16], lanes), got)
        tiles.append(got)
    listed = jnp.transpose(jnp.concatenate(tiles, axis=0))
    wide = [take_lanes(listed, (lane16 // 16) * 16 + f) for f in range(10)]
    dx = wide[0] - (lane16.astype(F32) + 0.5)
    ca, cb, cc, op = wide[2:6]
    fsc[0] = wide[1]
    fsc[1] = jnp.where(live, -0.5 * ca * dx * dx, -1e30)
    fsc[2] = cb * dx
    fsc[3] = 0.5 * cc
    fsc[4] = op
    for f in range(4):
        fsc[5 + f] = wide[6 + f]
    fsc[9] = ca * dx
    fsc[10] = cb
    fsc[11] = dx
    first_row = (s * TILE).astype(F32) + 0.5

    def alpha_rows(i, carry):
        at = pl.ds(pl.multiple_of(i * 16, 16), 16)
        low = pl.ds(pl.multiple_of(i * 16 + 128, 16), 16)
        r, ax, bx, c2, o = (fsc[n, at, :] for n in range(5))
        for row in range(16):
            dy = r - (first_row + float(row))
            raw = o * jnp.exp(ax - dy * (bx + c2 * dy))
            raws[row, at, :] = raw
            keep = jnp.log(1.0 - jnp.minimum(raw, ALPHA_MAX))
            high, rest = split(keep, 2)
            xsplit[at, row * 128 : (row + 1) * 128] = high
            xsplit[low, row * 128 : (row + 1) * 128] = rest
        return carry

    lax.fori_loop(0, 8, alpha_rows, 0)

    def compose_rows(i, carry):
        lanes = pl.ds(pl.multiple_of(i * 512, 512), 512)
        t4 = jnp.exp(dot(lower, xsplit[:, lanes]))
        for n in range(4):
            row = i * 4 + n
            t = t4[:, n * 128 : (n + 1) * 128]
            w = jnp.minimum(raws[row], ALPHA_MAX) * t
            trans[row] = t
            weights[row] = w
            for f in range(4):
                image[f, pl.ds(row, 1), :] = jnp.sum(w * fsc[5 + f], axis=0, keepdims=True)
        return carry

    lax.fori_loop(0, 4, compose_rows, 0)

    for n in range(3):
        send(image, n, halo_x, n, 3, (down, y))
        send(image, n, halo_x, 3 + n, 3, (up, y))
    stores[2].start()
    stores[3].start()

    def factor_rows(row, carry):
        raw = raws[row]
        moved = jnp.where(raw < ALPHA_MAX, raw, jnp.where(raw == ALPHA_MAX, 0.5 * raw, 0.0))
        raws[row] = moved / (1.0 - jnp.minimum(raw, ALPHA_MAX))
        trans[row] = trans[row] * moved
        return carry

    lax.fori_loop(0, 16, factor_rows, 0)
    wait_bytes(halo_x, 6, rsem.at[3])
    xs = [with_halo(halo_x, n, image[n]) for n in range(3)]
    x_stats = blur(xs + [v * v for v in xs] + [xs[n] * ys[n] for n in range(3)])
    grow = s * TILE - 8 + iota((32, 128), 0)
    share = jnp.where((grow >= 0) & (grow < height), -STRUCTURE_WEIGHT / (TILE * TILE), 0.0)
    pulls = []
    for n in range(3):
        mx, exx, exy = x_stats[n], x_stats[3 + n], x_stats[6 + n]
        my, eyy = y_stats[n], y_stats[3 + n]
        a1 = 2.0 * mx * my + STABLE_MEAN
        a2 = 2.0 * (exy - mx * my) + STABLE_SPREAD
        b1 = mx * mx + my * my + STABLE_MEAN
        b2 = (exx - mx * mx) + (eyy - my * my) + STABLE_SPREAD
        inv = share / (b1 * b2)
        ssim = a1 * a2 / (b1 * b2)
        d_exy = 2.0 * a1 * inv
        d_exx = -ssim * b1 * inv
        d_mx = 2.0 * (my * (a2 - a1) * inv - ssim * mx * (b2 - b1) * inv)
        pulls.append((d_mx, d_exx, d_exy))
    nine = [pulls[n][i] for i in range(3) for n in range(3)]
    tall = dot_exact(back_band, jnp.concatenate(nine, axis=1))
    flat = dot_exact(jnp.concatenate([tall[:, i * 128 : (i + 1) * 128] for i in range(9)], axis=0), across)
    for n in range(3):
        vx, vy = image[n], target_ref[n]
        diff = vx - vy
        smooth = (1.0 - STRUCTURE_WEIGHT) / (TILE * TILE) * diff / jnp.sqrt(diff * diff + SMOOTHING**2)
        b_mx, b_xx, b_xy = (flat[(i * 3 + n) * 16 : (i * 3 + n + 1) * 16] for i in range(3))
        gimage[n] = b_mx + 2.0 * vx * b_xx + vy * b_xy + smooth

    def pull_rows(i, carry):
        at = pl.ds(pl.multiple_of(i * 16, 16), 16)
        low = pl.ds(pl.multiple_of(i * 16 + 128, 16), 16)
        colors = [fsc[5 + f, at, :] for f in range(3)]
        for row in range(16):
            dw = sum(gimage[f, row : row + 1, :] * colors[f] for f in range(3))
            dweights[row, at, :] = dw
            high, rest = split(dw * weights[row, at, :], 2)
            xsplit[at, row * 128 : (row + 1) * 128] = high
            xsplit[low, row * 128 : (row + 1) * 128] = rest
        return carry

    lax.fori_loop(0, 8, pull_rows, 0)

    acc[...] = jnp.zeros_like(acc)

    def pull_alpha(i, carry):
        lanes = pl.ds(pl.multiple_of(i * 512, 512), 512)
        later = dot(upper, xsplit[:, lanes])
        sums = [0.0] * 6
        for n in range(4):
            row = i * 4 + n
            d_power = dweights[row] * trans[row] - later[:, n * 128 : (n + 1) * 128] * raws[row]
            dy = fsc[0] - (first_row + row.astype(F32))
            moved = d_power * dy
            w = weights[row]
            terms = [d_power, moved, moved * dy] + [w * gimage[f, pl.ds(row, 1), :] for f in range(3)]
            sums = [a + b for a, b in zip(sums, terms)]
        for n in range(6):
            acc[n] += sums[n]
        return carry

    lax.fori_loop(0, 4, pull_alpha, 0)
    s0, s1, s2 = acc[0], acc[1], acc[2]
    adx, cb, dx = fsc[9], fsc[10], fsc[11]
    grads = [
        -(adx * s0 + cb * s1),
        -(2.0 * fsc[3] * s1 + fsc[2] * s0),
        -0.5 * dx * dx * s0,
        -dx * s1,
        -0.5 * s2,
        s0 / fsc[4],
        acc[3],
        acc[4],
        acc[5],
    ]
    folded = sum(dot(jnp.concatenate(split(grads[f], 2), axis=1), fold[f]) for f in range(9))
    turned = jnp.transpose(folded)
    blocks = []
    for n in range(8):
        tile = jnp.broadcast_to(tile_from[n : n + 1], (16, 128))
        lanes = jnp.broadcast_to(entry_from[n : n + 1], (16, 128))
        put = take_lanes(turned[0:16], lanes)
        for t in range(1, 8):
            put = jnp.where(tile == t, take_lanes(turned[t * 16 : (t + 1) * 16], lanes), put)
        blocks.append(put)
    back2s[...] = jnp.transpose(jnp.concatenate(blocks, axis=0)).reshape(16, 8, 128)

    for at, dev in depth_peers:
        send(back2s, at, back2r, z, 4, dev)
    back2r[z] = back2s[z]
    wait_bytes(back2r, 15, rsem.at[4])
    for zq in range(4):
        for w in range(4):
            out = back2r[zq * 4 + w]
            for z4 in range(4):
                if z4 != w:
                    moved = pltpu.roll(back2r[zq * 4 + z4], ((z4 - w) * 32) % 128, axis=1)
                    out = jnp.where(quarter == z4, moved, out)
            back1s[w * 8 : (w + 1) * 8, zq, :] = out
    for at, dev in ring_peers:
        send(back1s, at, back1r, me, 5, dev)
    back1r[me] = back1s[me]
    wait_bytes(back1r, 31, rsem.at[5])
    for a in range(8):
        first = (a // 2) * 32 + a % 2
        rows = [back1r[v * 8 + a] for v in range(4)]
        for z4 in range(4):
            out = rows[z4]
            for v in range(4):
                if v != z4:
                    moved = pltpu.roll(rows[v], ((v - z4) * 32) % 128, axis=1)
                    out = jnp.where(quarter[0:4] == v, moved, out)
            sq[pl.ds(first + z4 * 2, 4, stride=8), :] = out
    sq[...] = jnp.transpose(sq[...])
    stores[4].start()

    wait_bytes(send1, 31, ssem.at[0])
    wait_bytes(halo_y, 6, ssem.at[1])
    wait_bytes(send2, 15, ssem.at[2])
    wait_bytes(halo_x, 6, ssem.at[3])
    wait_bytes(back2s, 15, ssem.at[4])
    wait_bytes(back1s, 31, ssem.at[5])
    for store in stores:
        store.wait()


def owner_kernel(
    grad_in, jac_in, inv_in, rend_in, depth_in,
    har_hbm, cen_hbm, lsc_hbm, rot_hbm, opa_hbm, rend_hbm, depth_hbm,
    grad_ref, jac_ref, inv_ref, rows_ref, har_ref, cen_ref, lsc_ref, rot_ref, opa_ref, sem,
):
    loads = [
        pltpu.make_async_copy(grad_in, grad_ref, sem.at[22]),
        pltpu.make_async_copy(jac_in, jac_ref, sem.at[23]),
        pltpu.make_async_copy(inv_in, inv_ref, sem.at[24]),
    ]
    copies = [
        pltpu.make_async_copy(rend_in, rend_hbm, sem.at[0]),
        pltpu.make_async_copy(depth_in, depth_hbm, sem.at[1]),
    ]
    for copy in loads + copies:
        copy.start()
    for load in loads:
        load.wait()
    du, dr, da, db, dc, do, *dcol = [grad_ref[pl.ds(f, 8, stride=16), :] for f in range(9)]
    jac = [jac_ref[n] for n in range(62)]
    conic = (da, db, dc)
    geo = [sum(conic[i] * jac[i * 10 + n] for i in range(3)) for n in range(10)]
    for n in range(3):
        geo[n] = geo[n] + sum(dcol[ch] * jac[30 + ch * 3 + n] for ch in range(3))
    ja, jx, jy, d_opaque = jac[39:43]
    geo[0] = geo[0] + du * ja
    geo[1] = geo[1] + dr * ja
    geo[2] = geo[2] + du * jx + dr * jy
    passed = [dcol[ch] * jac[43 + ch] for ch in range(3)]
    rows = [passed[ch] * jac[46 + i] for ch in range(3) for i in range(16)] + geo + [do * d_opaque]
    for i in range(59):
        rows_ref[i * 8 : (i + 1) * 8, :] = rows[i]
    for i in range(59, 64):
        rows_ref[i * 8 : (i + 1) * 8, :] = jnp.zeros((8, 128), F32)
    halves = [sum(rows_ref[pl.ds(v * 2 + j, 64, stride=8), :] for v in range(4)) for j in range(2)]
    count = har_hbm.shape[1]
    pieces = 4
    wide = count // pieces
    for piece in range(pieces):
        for h in range(piece * wide // 128, (piece + 1) * wide // 128):
            at = slice(h * 128, (h + 1) * 128)
            number = jnp.broadcast_to(inv_ref[h : h + 1, :], (64, 128))
            lanes = (number + 127) % 128
            out = jnp.where(number > 128, take_lanes(halves[1], lanes), take_lanes(halves[0], lanes))
            out = jnp.where(number > 0, out, 0.0)
            har_ref[:, at] = out[0:48]
            cen_ref[:, at] = out[48:51]
            lsc_ref[:, at] = out[51:54]
            rot_ref[:, at] = out[54:58]
            opa_ref[:, at] = out[58:59]
        part = pl.ds(piece * wide, wide)
        for n, (source, target) in enumerate((
            (har_ref, har_hbm), (cen_ref, cen_hbm), (lsc_ref, lsc_hbm), (rot_ref, rot_hbm), (opa_ref, opa_hbm)
        )):
            copy = pltpu.make_async_copy(source.at[:, part], target.at[:, part], sem.at[2 + piece * 5 + n])
            copy.start()
            copies.append(copy)
    for copy in copies:
        copy.wait()


def on_device(
    centers, log_scales, rotations, opacity, harmonics, cameras, send_index, tile_lists, counts, target
):
    strips = lax.axis_size("space")
    height = TILE * strips
    columns = target.shape[-1]
    count = centers.shape[1]
    hbm = pl.BlockSpec(memory_space=pltpu.HBM)
    index = jnp.swapaxes(send_index, 2, 3).reshape(2, strips)
    dma = pltpu.SemaphoreType.DMA

    def shape(*dims):
        return jax.ShapeDtypeStruct(dims, F32)

    params = [VMEM((48, count), F32), VMEM((3, count), F32), VMEM((3, count), F32), VMEM((4, count), F32), VMEM((1, count), F32)]
    rendered, inverse_depth, jacobian, inverse, grads = pl.pallas_call(
        functools.partial(step_kernel, height, columns),
        out_shape=[
            shape(3, 16, 128),
            shape(16, 128),
            shape(62, 8, 128),
            jax.ShapeDtypeStruct((32, 128), jnp.int32),
            shape(128, 128),
        ],
        in_specs=[hbm] * 10,
        out_specs=[hbm] * 5,
        scratch_shapes=params + [
            VMEM((4, 3), F32),
            VMEM((2, 128), jnp.int32),
            VMEM((8, 128), jnp.int32),
            VMEM((1, 8), jnp.int32),
            VMEM((3, 16, 128), F32),
            VMEM((16, count), F32),
            VMEM((128, 128), F32),
            VMEM((128, 128), F32),
            VMEM((32, 4, 128), F32),
            VMEM((32, 4, 128), F32),
            VMEM((16, 8, 128), F32),
            VMEM((16, 8, 128), F32),
            VMEM((9, 256, 128), BF16),
            VMEM((6, 16, 128), F32),
            VMEM((6, 16, 128), F32),
            VMEM((16, 128, 128), F32),
            VMEM((16, 128, 128), F32),
            VMEM((16, 128, 128), F32),
            VMEM((16, 128, 128), F32),
            VMEM((256, 2048), BF16),
            VMEM((6, 128, 128), F32),
            VMEM((4, 16, 128), F32),
            VMEM((3, 16, 128), F32),
            VMEM((12, 128, 128), F32),
            VMEM((16, 8, 128), F32),
            VMEM((16, 8, 128), F32),
            VMEM((32, 4, 128), F32),
            VMEM((32, 4, 128), F32),
            VMEM((62, 8, 128), F32),
            VMEM((32, 128), jnp.int32),
            dma((15,)),
            dma((6,)),
            dma((6,)),
        ],
        compiler_params=pltpu.CompilerParams(
            collective_id=0, has_side_effects=True, vmem_limit_bytes=60 * 2**20
        ),
        name="render_step",
    )(
        harmonics.reshape(48, count),
        centers,
        log_scales,
        rotations,
        opacity.reshape(1, count),
        cameras,
        index,
        tile_lists[0],
        counts,
        target[0],
    )
    d_har, d_cen, d_lsc, d_rot, d_opa, rendered, inverse_depth = pl.pallas_call(
        owner_kernel,
        out_shape=[
            shape(48, count), shape(3, count), shape(3, count), shape(4, count), shape(1, count),
            shape(3, 16, 128), shape(16, 128),
        ],
        in_specs=[hbm] * 5,
        out_specs=[hbm] * 7,
        scratch_shapes=[
            VMEM((128, 128), F32),
            VMEM((62, 8, 128), F32),
            VMEM((32, 128), jnp.int32),
            VMEM((512, 128), F32),
        ]
        + params
        + [dma((25,))],
        compiler_params=pltpu.CompilerParams(vmem_limit_bytes=60 * 2**20),
        name="owner_pull",
    )(grads, jacobian, inverse, rendered, inverse_depth)
    return (
        rendered[None],
        inverse_depth[None],
        d_cen,
        d_lsc,
        d_rot,
        d_opa.reshape(count),
        d_har.reshape(3, 16, count),
    )


def solution(mesh):
    return jax.shard_map(
        on_device,
        mesh=mesh,
        in_specs=(
            P(None, ("space", "view")),
            P(None, ("space", "view")),
            P(None, ("space", "view")),
            P(("space", "view")),
            P(None, None, ("space", "view")),
            P(),
            P("space", "view", None, None),
            P("space", None, None),
            P("space", None),
            P("view", None, "space", None),
        ),
        out_specs=(
            P("view", None, "space", None),
            P("view", "space", None),
            P(None, ("space", "view")),
            P(None, ("space", "view")),
            P(None, ("space", "view")),
            P(("space", "view")),
            P(None, None, ("space", "view")),
        ),
        check_vma=False,
    )
```

time: 70.1 us -> 54.4 us (0.78)
  Pallas kernels: 62 us -> 53.6 us
  local copies, waits for them, and re-layouts: 6.92 us -> 0 us
    unnamed x21 -> x0, local copies, waits for them, and re-layouts: 6.92 us -> none
    pallas_call x1, Pallas kernels: 57.4 us -> 50.9 us  [on_device(): pl.pallas_call(functools.partial(step_kernel, height, columns), out_shape...]
    pallas_call x1, Pallas kernels: 4.63 us -> 2.66 us  [on_device(): pl.pallas_call(owner_kernel, out_shape=[shape(48, count), shape(3, count)...]
where the time goes in v2:
time: 54.4 us; the launch traced here: 54.2 us
  Pallas kernels  53.6 us (99%)
  between operations  0.64 us (1%)
    pallas_call x1, Pallas kernels, on_device(): pl.pallas_call(functools.partial(step_kernel, height, columns), out_shape...  50.9 us
    pallas_call x1, Pallas kernels, on_device(): pl.pallas_call(owner_kernel, out_shape=[shape(48, count), shape(3, count)...  2.66 us

profile of v2, /device:TPU:1, one launch (start us, length us, event | category | flops | bytes accessed | tf_op | source)
XLA Modules:
  0.0 54.2 jit_solution(5078742730476181533)
XLA Ops:
  0.6 50.9 %render_step.1 = (f32[3,16,128]{2,1,0:T(8,128)}, f32[16,128]{1,0:T(8,128)}, f32[62,8,128]{2,1,0:T(8,128)}, s32[32,128]{1,0:T(8,128)}, f32[128,128]{1,0:T(8,128)}) custom-call(f32[48,4096]{1,0:T(8,128)} %bitcast.11, f32[3,4096]{1,0:T(4,128)} %cen_hbm.1, f32[3,4096]{1,0:T(4,128)} %lsc_hbm.1, f32[4,4096]{1,0:T(4,128)} %rot_hbm.1, f32[1,4096]{1,0:T(1,128)} %bitcast.13, ...), custom_call_target="tpu_custom_call" | custom-call | tf_op jit(solution)/shard_map/render_step/pallas_call | solution.py:649
  51.6 2.7 %owner_pull.1 = (f32[48,4096]{1,0:T(8,128)}, f32[3,4096]{1,0:T(4,128)}, f32[3,4096]{1,0:T(4,128)}, f32[4,4096]{1,0:T(4,128)}, f32[1,4096]{1,0:T(1,128)}, /*index=5*/f32[3,16,128]{2,1,0:T(8,128)}, f32[16,128]{1,0:T(8,128)}) custom-call(f32[128,128]{1,0:T(8,128)} %get-tuple-element.19.grad_in, f32[62,8,128]{2,1,0:T(8,128)} %get-tuple-element.20.jac_in, ...), custom_call_target="tpu_custom_call" | custom-call | tf_op jit(solution)/shard_map/owner_pull/pallas_call | solution.py:711

commit v3 on v2

--- a/solution.py
+++ b/solution.py
@@ -43,6 +43,8 @@
 VMEM = pltpu.VMEM
 EXACT = lax.Precision.HIGHEST
 
+SEAT = [0, 1, 2, 3, 4, 8, 9, 10, 11, 12]
+
 
 def harmonic_basis(ux, uy, uz):
     xx, yy, zz = ux * ux, uy * uy, uz * uz
@@ -157,7 +159,7 @@
             jnp.broadcast_to(first[i : i + 1], (8, 128)),
             jnp.broadcast_to(second[i : i + 1], (8, 128)),
         )
-        for i in range(59)
+        for i in range(first.shape[0])
     ]
 
 
@@ -169,51 +171,49 @@
 def step_kernel(
     height, columns,
     har_hbm, cen_hbm, lsc_hbm, rot_hbm, opa_hbm, cam_hbm, idx_hbm, list_hbm, cnt_hbm, target_hbm,
-    rend_hbm, depth_hbm, jac_hbm, inv_hbm, grad_hbm,
+    rend_hbm, depth_hbm, inv_hbm, grad_hbm,
     har_ref, cen_ref, lsc_ref, rot_ref, opa_ref, cam_ref, idx_ref, list_ref, cnt_ref, target_ref,
     small, feat, sq, send1, recv1, send2, recv2, fold,
     halo_x, halo_y, raws, trans, weights, dweights, xsplit, acc, image, gimage, fsc,
-    back2s, back2r, back1s, back1r, jac_ref, inv_ref, lsem, ssem, rsem,
+    back2s, back2r, back1s, back1r, inv_ref, rows_ref, grad_ref, turn, lsem, ssem, rsem,
 ):
     s = lax.axis_index("space")
     y = lax.axis_index("view")
-    x = s // 32
-    z = (s // 2) % 16
-    c = s % 2
+    x = lax.div(s, 32)
+    z = lax.rem(lax.div(s, 2), 16)
+    c = lax.rem(s, 2)
     q = x * 2 + c
-    up = (s + 127) % 128
-    down = (s + 1) % 128
-
+    up = lax.rem(s + 127, 128)
+    down = lax.rem(s + 1, 128)
     quarter = iota((8, 128), 1) // 32
 
-    def place(q2, z2):
-        return ((q2 // 2) * 16 + z2) * 2 + q2 % 2
-
     ring_peers = []
-    for e in range(1, 32):
-        q2, y2 = (q + e) % 8, (y + e // 8) % 4
-        ring_peers.append((y2 * 8 + q2, (place(q2, z), y2)))
+    xs = [lax.rem(x + d, 4) for d in range(4)]
+    ys = [lax.rem(y + d, 4) for d in range(4)]
+    for dx, dy in sorted(((a, b) for a in range(4) for b in range(4)), key=lambda d: -(d[0] != 0) - (d[1] != 0) - (d[0] == 2) - (d[1] == 2)):
+        for c2 in (1 - c, c):
+            if dx or dy or c2 is not c:
+                ring_peers.append((ys[dy] * 8 + xs[dx] * 2 + c2, (xs[dx] * 32 + z * 2 + c2, ys[dy])))
     depth_peers = []
     for d in (8, 7, 9, 6, 10, 5, 11, 4, 12, 3, 13, 2, 14, 1, 15):
-        z2 = (z + d) % 16
-        depth_peers.append((z2, (place(q, z2), y)))
-
-    barrier = pltpu.get_barrier_semaphore()
-    for _, dev in depth_peers + ring_peers + [(0, ((s + 2 * c + 127) % 128, y))]:
-        pl.semaphore_signal(barrier, inc=1, device_id=dev, device_id_type=MESH)
-    loads = [
-        pltpu.make_async_copy(source, place_in, lsem.at[n])
-        for n, (source, place_in) in enumerate((
-            (idx_hbm, idx_ref), (har_hbm, har_ref), (cen_hbm, cen_ref), (lsc_hbm, lsc_ref), (rot_hbm, rot_ref),
-            (opa_hbm, opa_ref), (cam_hbm, cam_ref), (list_hbm, list_ref), (cnt_hbm, cnt_ref), (target_hbm, target_ref),
-        ))
-    ]
+        z2 = lax.rem(z + d, 16)
+        depth_peers.append((z2, (x * 32 + z2 * 2 + c, y)))
+
+    pairs = (
+        (har_hbm, har_ref), (idx_hbm, idx_ref), (cen_hbm, cen_ref), (lsc_hbm, lsc_ref), (rot_hbm, rot_ref),
+        (opa_hbm, opa_ref), (cam_hbm, cam_ref), (list_hbm, list_ref), (cnt_hbm, cnt_ref), (target_hbm, target_ref),
+    )
+    loads = [pltpu.make_async_copy(a, b, lsem.at[n]) for n, (a, b) in enumerate(pairs)]
     for load in loads:
         load.start()
-    for load in loads:
+    barrier = pltpu.get_barrier_semaphore()
+    for _, dev in depth_peers + ring_peers + [(0, (lax.rem(s + 2 * c + 127, 128), y))]:
+        pl.semaphore_signal(barrier, inc=1, device_id=dev, device_id_type=MESH)
+    feat[...] = jnp.zeros_like(feat)
+    small[...] = jnp.zeros_like(small)
+
+    for load in loads[1:7]:
         load.wait()
-
-    small[...] = jnp.zeros_like(small)
     small[0:3, :] = cen_ref[...]
     small[3:6, :] = lsc_ref[...]
     small[6:10, :] = rot_ref[...]
@@ -222,24 +222,30 @@
     chunk_of = [jnp.broadcast_to(number[j : j + 1] // 128, (64, 128)) for j in range(2)]
     lane_of = [jnp.broadcast_to(number[j : j + 1] % 128, (64, 128)) for j in range(2)]
 
-    def gather_chunk(i, carry):
-        at = pl.ds(pl.multiple_of(i * 128, 128), 128)
-        block = jnp.concatenate([har_ref[:, at], small[:, at]], axis=0)
-        return tuple(jnp.where(chunk_of[j] == i, take_lanes(block, lane_of[j]), carry[j]) for j in range(2))
-
-    zero = jnp.zeros((64, 128), F32)
-    picked = lax.fori_loop(0, har_ref.shape[1] // 128, gather_chunk, (zero, zero), unroll=4)
-    prm = spread_params(*picked)
+    def gather(ref):
+        rows = ref.shape[0]
+
+        def gather_chunk(i, carry):
+            block = ref[:, pl.ds(pl.multiple_of(i * 128, 128), 128)]
+            return tuple(
+                jnp.where(chunk_of[j][0:rows] == i, take_lanes(block, lane_of[j][0:rows]), carry[j]) for j in range(2)
+            )
+
+        zero = jnp.zeros((rows, 128), F32)
+        return spread_params(*lax.fori_loop(0, ref.shape[1] // 128, gather_chunk, (zero, zero), unroll=8))
+
+    prm = gather(small)
     camera = view_camera(cam_ref)
-    center, log_scale, quaternion = prm[48:51], prm[51:54], prm[54:58]
+    center, log_scale, quaternion = prm[0:3], prm[3:6], prm[6:10]
     u, r, ca, cb, cc, iz = geometry(center, log_scale, quaternion, camera, height, columns)
-    opaque = 1.0 / (1.0 + jnp.exp(-prm[58]))
+    opaque = 1.0 / (1.0 + jnp.exp(-prm[10]))
     basis = directions(center, camera)
-    raw_colors = [raw_color(prm, basis, ch) for ch in range(3)]
+    loads[0].wait()
+    har = gather(har_ref)
+    raw_colors = [raw_color(har, basis, ch) for ch in range(3)]
     features = [u, r, ca, cb, cc, opaque] + [jnp.maximum(0.0, v) for v in raw_colors] + [iz]
-    feat[...] = jnp.zeros_like(feat)
     for f in range(10):
-        feat[pl.ds(f, 8, stride=16), :] = features[f]
+        feat[pl.ds(SEAT[f], 8, stride=16), :] = features[f]
     sq[...] = jnp.transpose(feat[...])
     for a in range(8):
         first = (a // 2) * 32 + a % 2
@@ -252,6 +258,8 @@
                     out = jnp.where(quarter[0:4] == z4, moved, out)
             send1[v * 8 + a] = out
 
+    for load in loads[7:10]:
+        load.wait()
     pl.semaphore_wait(barrier, 47)
 
     def send(src, src_at, dst, dst_at, stage, dev):
@@ -264,80 +272,54 @@
     for at, dev in ring_peers:
         send(send1, at, recv1, me, 0, dev)
     recv1[me] = send1[me]
-    for n in range(3):
-        send(target_ref, n, halo_y, n, 1, (down, y))
-        send(target_ref, n, halo_y, 3 + n, 1, (up, y))
-
-    _, pull = jax.vjp(
-        lambda *a: geometry(*a, camera, height, columns)[2:5], center, log_scale, quaternion
-    )
-    one, none = jnp.ones((8, 128), F32), jnp.zeros((8, 128), F32)
-    jac = []
-    for i in range(3):
-        d_center, d_scale, d_turn = pull(tuple(one if i == n else none for n in range(3)))
-        jac += list(d_center) + list(d_scale) + list(d_turn)
-    passed = [jnp.where(v > 0.0, 1.0, jnp.where(v == 0.0, 0.5, 0.0)) for v in raw_colors]
-    for ch in range(3):
-        _, pull = jax.vjp(lambda a: raw_color(prm, directions(a, camera), ch), center)
-        jac += [passed[ch] * v for v in pull(one)[0]]
-    shift = [center[i] - camera[i] for i in range(2)]
-    jac += [FOCAL_LENGTH * iz] + [-FOCAL_LENGTH * v * iz * iz for v in shift]
-    jac += [opaque * (1.0 - opaque)] + passed + basis
-    for n, value in enumerate(jac):
-        jac_ref[n] = value
+    send(target_ref, pl.ds(0, 3), halo_y, pl.ds(0, 3), 1, (down, y))
+    send(target_ref, pl.ds(0, 3), halo_y, pl.ds(3, 3), 1, (up, y))
 
     row128 = iota((128, 128), 0)
     lane128 = iota((128, 128), 1)
-    columns_of = jnp.transpose(jnp.concatenate([number.astype(F32)] * 64, axis=0)).astype(jnp.int32)
-    total = jnp.zeros((32, 128), F32)
-    for j in range(2):
-        hit = chunk_of[j][0:32] == iota((32, 128), 0)
-        value = jnp.where(hit, (iota((32, 128), 1) + (1 + j * 128)).astype(F32), 0.0).astype(BF16)
-        total = total + dot(value, one_hot(columns_of[:, j : j + 1] % 128 == lane128))
-    inv_ref[...] = total.astype(jnp.int32)
+    row16, lane16 = row128, lane128
+    slot = list_ref[...]
+    source = (slot // 2) % 128
+    block_of = (source // 2) % 16
+    lane_in = (slot % 2) * 32 + (slot // 256) * 8 + (source // 32) * 2 + source % 2
+    lane_cols = jnp.transpose(jnp.concatenate([lane_in.astype(F32)] * 16, axis=0)).astype(jnp.int32)
+    inverse = jnp.zeros((32, 128), F32)
+    for t in range(8):
+        hit = jnp.broadcast_to(block_of[t : t + 1], (16, 128)) == iota((16, 128), 0)
+        value = jnp.concatenate(
+            [jnp.where(hit, float(t), 0.0), jnp.where(hit, iota((16, 128), 1).astype(F32), 0.0)], axis=0
+        ).astype(BF16)
+        inverse = inverse + dot(value, one_hot(lane_cols[:, t : t + 1] == lane128 % 64))
+    inverse = inverse.astype(jnp.int32)
+    tile_from, entry_from = inverse[0:16], inverse[16:32]
     stores = [
-        pltpu.make_async_copy(jac_ref, jac_hbm, lsem.at[10]),
-        pltpu.make_async_copy(inv_ref, inv_hbm, lsem.at[11]),
-        pltpu.make_async_copy(image.at[pl.ds(0, 3)], rend_hbm, lsem.at[12]),
-        pltpu.make_async_copy(image.at[3], depth_hbm, lsem.at[13]),
-        pltpu.make_async_copy(sq, grad_hbm, lsem.at[14]),
+        pltpu.make_async_copy(inv_ref, inv_hbm, lsem.at[10]),
+        pltpu.make_async_copy(image.at[pl.ds(0, 3)], rend_hbm, lsem.at[11]),
+        pltpu.make_async_copy(image.at[3], depth_hbm, lsem.at[12]),
+        pltpu.make_async_copy(grad_ref, grad_hbm, lsem.at[13]),
     ]
-    stores[0].start()
-    stores[1].start()
-
-    slot = list_ref[...]
-    block_of = (slot // 256) * 2 + slot % 2
-    source = (slot // 2) % 128
-    lane_in = ((source // 2) % 16) * 8 + (source // 32) * 2 + source % 2
-    lane_cols = jnp.transpose(jnp.concatenate([lane_in.astype(F32)] * 16, axis=0)).astype(jnp.int32)
-    inverse = jnp.zeros((16, 128), F32)
-    for t in range(8):
-        hit = jnp.broadcast_to(block_of[t : t + 1], (8, 128)) == iota((8, 128), 0)
-        value = jnp.concatenate(
-            [jnp.where(hit, float(t), 0.0), jnp.where(hit, iota((8, 128), 1).astype(F32), 0.0)], axis=0
-        ).astype(BF16)
-        inverse = inverse + dot(value, one_hot(lane_cols[:, t : t + 1] == lane128))
-    inverse = inverse.astype(jnp.int32)
-    tile_from, entry_from = inverse[0:8], inverse[8:16]
     wait_bytes(recv1, 31, rsem.at[0])
     for zq in range(4):
-        rows = [recv1[w * 8 : (w + 1) * 8, zq, :] for w in range(4)]
-        for z4 in range(4):
-            out = rows[z4]
-            for w in range(4):
-                if w != z4:
-                    out = jnp.where(quarter == w, pltpu.roll(rows[w], ((w - z4) * 32) % 128, axis=1), out)
-            send2[zq * 4 + z4] = out
+        for w in range(4):
+            turn[zq * 32 + w * 8 : zq * 32 + w * 8 + 8, :] = recv1[w * 8 : (w + 1) * 8, zq, :]
+    flat = jnp.transpose(turn[...])
+    for z4 in range(4):
+        rows = [flat[z4 * 32 + (n % 2) * 16 + (n // 2) * 8 :][0:8] for n in range(4)]
+        for zq in range(4):
+            out = rows[zq]
+            for n in range(4):
+                if n != zq:
+                    out = jnp.where(quarter == n, pltpu.roll(rows[n], ((n - zq) * 32) % 128, axis=1), out)
+            send2[zq * 4 + z4] = out[0:5]
 
     for at, dev in depth_peers:
         send(send2, at, recv2, z, 2, dev)
     recv2[z] = send2[z]
 
-    row16, lane16 = row128, lane128
     for f in range(9):
-        shrink = one_hot(lane16 == (row16 // 16) * 16 + f)
+        shrink = one_hot(row16 == (lane16 // 16) * 16 + SEAT[f])
         for n in range(2):
-            fold[f, n * 128 : (n + 1) * 128, :] = shrink
+            fold[:, (f * 2 + n) * 128 : (f * 2 + n + 1) * 128] = shrink
     lower = one_hot(lane16 < row16)
     upper = one_hot(lane16 > row16)
     lower = jnp.concatenate([lower, lower], axis=1)
@@ -374,17 +356,18 @@
 
     wait_bytes(recv2, 15, rsem.at[2])
 
-    rt = jnp.transpose(recv2[...].reshape(128, 128))
+    got_z = [jnp.concatenate([recv2[n], jnp.zeros((3, 128), F32)], axis=0) for n in range(16)]
     tiles = []
     for t in range(8):
-        block = jnp.broadcast_to(block_of[t : t + 1], (16, 128))
-        lanes = jnp.broadcast_to(lane_in[t : t + 1], (16, 128))
-        got = take_lanes(rt[0:16], lanes)
-        for n in range(1, 8):
-            got = jnp.where(block == n, take_lanes(rt[n * 16 : (n + 1) * 16], lanes), got)
-        tiles.append(got)
+        block = jnp.broadcast_to(block_of[t : t + 1], (8, 128))
+        lanes = jnp.broadcast_to(lane_in[t : t + 1], (8, 128))
+        for half in range(2):
+            got = take_lanes(got_z[0], lanes + half * 64)
+            for n in range(1, 16):
+                got = jnp.where(block == n, take_lanes(got_z[n], lanes + half * 64), got)
+            tiles.append(got)
     listed = jnp.transpose(jnp.concatenate(tiles, axis=0))
-    wide = [take_lanes(listed, (lane16 // 16) * 16 + f) for f in range(10)]
+    wide = [take_lanes(listed, (lane16 // 16) * 16 + SEAT[f]) for f in range(10)]
     dx = wide[0] - (lane16.astype(F32) + 0.5)
     ca, cb, cc, op = wide[2:6]
     fsc[0] = wide[1]
@@ -399,25 +382,14 @@
     fsc[11] = dx
     first_row = (s * TILE).astype(F32) + 0.5
 
-    def alpha_rows(i, carry):
-        at = pl.ds(pl.multiple_of(i * 16, 16), 16)
-        low = pl.ds(pl.multiple_of(i * 16 + 128, 16), 16)
-        r, ax, bx, c2, o = (fsc[n, at, :] for n in range(5))
-        for row in range(16):
-            dy = r - (first_row + float(row))
-            raw = o * jnp.exp(ax - dy * (bx + c2 * dy))
-            raws[row, at, :] = raw
-            keep = jnp.log(1.0 - jnp.minimum(raw, ALPHA_MAX))
-            high, rest = split(keep, 2)
-            xsplit[at, row * 128 : (row + 1) * 128] = high
-            xsplit[low, row * 128 : (row + 1) * 128] = rest
-        return carry
-
-    lax.fori_loop(0, 8, alpha_rows, 0)
-
-    def compose_rows(i, carry):
-        lanes = pl.ds(pl.multiple_of(i * 512, 512), 512)
-        t4 = jnp.exp(dot(lower, xsplit[:, lanes]))
+    for i in range(4):
+        keeps = []
+        for row in range(i * 4, i * 4 + 4):
+            dy = fsc[0] - (first_row + float(row))
+            raw = fsc[4] * jnp.exp(fsc[1] - dy * (fsc[2] + fsc[3] * dy))
+            raws[row] = raw
+            keeps.append(jnp.concatenate(split(jnp.log(1.0 - jnp.minimum(raw, ALPHA_MAX)), 2), axis=0))
+        t4 = jnp.exp(dot(lower, jnp.concatenate(keeps, axis=1)))
         for n in range(4):
             row = i * 4 + n
             t = t4[:, n * 128 : (n + 1) * 128]
@@ -425,16 +397,12 @@
             trans[row] = t
             weights[row] = w
             for f in range(4):
-                image[f, pl.ds(row, 1), :] = jnp.sum(w * fsc[5 + f], axis=0, keepdims=True)
-        return carry
-
-    lax.fori_loop(0, 4, compose_rows, 0)
-
-    for n in range(3):
-        send(image, n, halo_x, n, 3, (down, y))
-        send(image, n, halo_x, 3 + n, 3, (up, y))
+                image[f, row : row + 1, :] = jnp.sum(w * fsc[5 + f], axis=0, keepdims=True)
+
+    send(image, pl.ds(0, 3), halo_x, pl.ds(0, 3), 3, (down, y))
+    send(image, pl.ds(0, 3), halo_x, pl.ds(3, 3), 3, (up, y))
+    stores[1].start()
     stores[2].start()
-    stores[3].start()
 
     def factor_rows(row, carry):
         raw = raws[row]
@@ -473,39 +441,25 @@
         b_mx, b_xx, b_xy = (flat[(i * 3 + n) * 16 : (i * 3 + n + 1) * 16] for i in range(3))
         gimage[n] = b_mx + 2.0 * vx * b_xx + vy * b_xy + smooth
 
-    def pull_rows(i, carry):
-        at = pl.ds(pl.multiple_of(i * 16, 16), 16)
-        low = pl.ds(pl.multiple_of(i * 16 + 128, 16), 16)
-        colors = [fsc[5 + f, at, :] for f in range(3)]
-        for row in range(16):
-            dw = sum(gimage[f, row : row + 1, :] * colors[f] for f in range(3))
-            dweights[row, at, :] = dw
-            high, rest = split(dw * weights[row, at, :], 2)
-            xsplit[at, row * 128 : (row + 1) * 128] = high
-            xsplit[low, row * 128 : (row + 1) * 128] = rest
-        return carry
-
-    lax.fori_loop(0, 8, pull_rows, 0)
-
     acc[...] = jnp.zeros_like(acc)
-
-    def pull_alpha(i, carry):
-        lanes = pl.ds(pl.multiple_of(i * 512, 512), 512)
-        later = dot(upper, xsplit[:, lanes])
+    for i in range(4):
+        dws, products = [], []
+        for row in range(i * 4, i * 4 + 4):
+            dw = sum(gimage[f, row : row + 1, :] * fsc[5 + f] for f in range(3))
+            dws.append(dw)
+            products.append(jnp.concatenate(split(dw * weights[row], 2), axis=0))
+        later = dot(upper, jnp.concatenate(products, axis=1))
         sums = [0.0] * 6
         for n in range(4):
             row = i * 4 + n
-            d_power = dweights[row] * trans[row] - later[:, n * 128 : (n + 1) * 128] * raws[row]
-            dy = fsc[0] - (first_row + row.astype(F32))
-            moved = d_power * dy
-            w = weights[row]
-            terms = [d_power, moved, moved * dy] + [w * gimage[f, pl.ds(row, 1), :] for f in range(3)]
+            d_power = dws[n] * trans[row] - later[:, n * 128 : (n + 1) * 128] * raws[row]
+            moved = d_power * (fsc[0] - (first_row + float(row)))
+            dy = fsc[0] - (first_row + float(row))
+            terms = [d_power, moved, moved * dy]
+            terms += [weights[row] * gimage[f, row : row + 1, :] for f in range(3)]
             sums = [a + b for a, b in zip(sums, terms)]
         for n in range(6):
             acc[n] += sums[n]
-        return carry
-
-    lax.fori_loop(0, 4, pull_alpha, 0)
     s0, s1, s2 = acc[0], acc[1], acc[2]
     adx, cb, dx = fsc[9], fsc[10], fsc[11]
     grads = [
@@ -519,30 +473,64 @@
         acc[4],
         acc[5],
     ]
-    folded = sum(dot(jnp.concatenate(split(grads[f], 2), axis=1), fold[f]) for f in range(9))
-    turned = jnp.transpose(folded)
-    blocks = []
-    for n in range(8):
-        tile = jnp.broadcast_to(tile_from[n : n + 1], (16, 128))
-        lanes = jnp.broadcast_to(entry_from[n : n + 1], (16, 128))
-        put = take_lanes(turned[0:16], lanes)
-        for t in range(1, 8):
-            put = jnp.where(tile == t, take_lanes(turned[t * 16 : (t + 1) * 16], lanes), put)
-        blocks.append(put)
-    back2s[...] = jnp.transpose(jnp.concatenate(blocks, axis=0)).reshape(16, 8, 128)
+    parts = [part for f in range(9) for part in split(grads[f], 2)]
+    turned = lax.dot_general(
+        fold[...], jnp.concatenate(parts, axis=1), (((1,), (1,)), ((), ())), preferred_element_type=F32
+    )
+    for n in range(16):
+        tile = jnp.broadcast_to(tile_from[n : n + 1], (8, 128))
+        lanes = jnp.broadcast_to(entry_from[n : n + 1], (8, 128))
+        halves = []
+        for half in range(2):
+            put = take_lanes(turned[half * 8 : half * 8 + 8], lanes)
+            for t in range(1, 8):
+                at = t * 16 + half * 8
+                put = jnp.where(tile == t, take_lanes(turned[at : at + 8], lanes), put)
+            halves.append(put)
+        back2s[n] = jnp.where(quarter < 2, halves[0], halves[1])[0:5]
 
     for at, dev in depth_peers:
         send(back2s, at, back2r, z, 4, dev)
     back2r[z] = back2s[z]
+    _, pull = jax.vjp(
+        lambda *a: geometry(*a, camera, height, columns)[2:5], center, log_scale, quaternion
+    )
+    one, none = jnp.ones((8, 128), F32), jnp.zeros((8, 128), F32)
+    jac = []
+    for i in range(3):
+        d_center, d_scale, d_turn = pull(tuple(one if i == n else none for n in range(3)))
+        jac += list(d_center) + list(d_scale) + list(d_turn)
+    passed = [jnp.where(v > 0.0, 1.0, jnp.where(v == 0.0, 0.5, 0.0)) for v in raw_colors]
+    for ch in range(3):
+        _, pull = jax.vjp(lambda a: raw_color(har, directions(a, camera), ch), center)
+        jac += [passed[ch] * v for v in pull(one)[0]]
+    shift = [center[i] - camera[i] for i in range(2)]
+    jac += [FOCAL_LENGTH * iz] + [-FOCAL_LENGTH * v * iz * iz for v in shift]
+    jac += [opaque * (1.0 - opaque)]
+
+    columns_of = jnp.transpose(jnp.concatenate([number.astype(F32)] * 64, axis=0)).astype(jnp.int32)
+    total = jnp.zeros((32, 128), F32)
+    for j in range(2):
+        hit = chunk_of[j][0:32] == iota((32, 128), 0)
+        value = jnp.where(hit, (iota((32, 128), 1) + (1 + j * 128)).astype(F32), 0.0).astype(BF16)
+        total = total + dot(value, one_hot(columns_of[:, j : j + 1] % 128 == lane128))
+    inv_ref[...] = total.astype(jnp.int32)
+    stores[0].start()
     wait_bytes(back2r, 15, rsem.at[4])
+    back_z = [jnp.concatenate([back2r[n], jnp.zeros((3, 128), F32)], axis=0) for n in range(16)]
+    for z4 in range(4):
+        for n in range(4):
+            out = back_z[n * 4 + z4]
+            for zq in range(4):
+                if zq != n:
+                    moved = pltpu.roll(back_z[zq * 4 + z4], ((zq - n) * 32) % 128, axis=1)
+                    out = jnp.where(quarter == zq, moved, out)
+            at = z4 * 32 + (n % 2) * 16 + (n // 2) * 8
+            turn[at : at + 8, :] = out
+    turn[...] = jnp.transpose(turn[...])
     for zq in range(4):
         for w in range(4):
-            out = back2r[zq * 4 + w]
-            for z4 in range(4):
-                if z4 != w:
-                    moved = pltpu.roll(back2r[zq * 4 + z4], ((z4 - w) * 32) % 128, axis=1)
-                    out = jnp.where(quarter == z4, moved, out)
-            back1s[w * 8 : (w + 1) * 8, zq, :] = out
+            back1s[w * 8 : (w + 1) * 8, zq, :] = turn[zq * 32 + w * 8 : zq * 32 + w * 8 + 8, :]
     for at, dev in ring_peers:
         send(back1s, at, back1r, me, 5, dev)
     back1r[me] = back1s[me]
@@ -557,8 +545,25 @@
                     moved = pltpu.roll(rows[v], ((v - z4) * 32) % 128, axis=1)
                     out = jnp.where(quarter[0:4] == v, moved, out)
             sq[pl.ds(first + z4 * 2, 4, stride=8), :] = out
-    sq[...] = jnp.transpose(sq[...])
-    stores[4].start()
+    turn[...] = jnp.transpose(sq[...])
+    du, dr, da, db, dc, do, *dcol = [turn[pl.ds(SEAT[f], 8, stride=16), :] for f in range(9)]
+    conic = (da, db, dc)
+    geo = [sum(conic[i] * jac[i * 10 + n] for i in range(3)) for n in range(10)]
+    for n in range(3):
+        geo[n] = geo[n] + sum(dcol[ch] * jac[30 + ch * 3 + n] for ch in range(3))
+    ja, jx, jy, d_opaque = jac[39:43]
+    geo[0] = geo[0] + du * ja
+    geo[1] = geo[1] + dr * ja
+    geo[2] = geo[2] + du * jx + dr * jy
+    shown = [dcol[ch] * passed[ch] for ch in range(3)]
+    rows = [shown[ch] * basis[i] for ch in range(3) for i in range(16)] + geo + [do * d_opaque]
+    for i in range(59):
+        rows_ref[i * 8 : (i + 1) * 8, :] = rows[i]
+    for i in range(59, 64):
+        rows_ref[i * 8 : (i + 1) * 8, :] = none
+    for j in range(2):
+        grad_ref[j] = sum(rows_ref[pl.ds(v * 2 + j, 64, stride=8), :] for v in range(4))
+    stores[3].start()
 
     wait_bytes(send1, 31, ssem.at[0])
     wait_bytes(halo_y, 6, ssem.at[1])
@@ -571,14 +576,13 @@
 
 
 def owner_kernel(
-    grad_in, jac_in, inv_in, rend_in, depth_in,
+    grad_in, inv_in, rend_in, depth_in,
     har_hbm, cen_hbm, lsc_hbm, rot_hbm, opa_hbm, rend_hbm, depth_hbm,
-    grad_ref, jac_ref, inv_ref, rows_ref, har_ref, cen_ref, lsc_ref, rot_ref, opa_ref, sem,
+    grad_ref, inv_ref, har_ref, cen_ref, lsc_ref, rot_ref, opa_ref, sem,
 ):
     loads = [
         pltpu.make_async_copy(grad_in, grad_ref, sem.at[22]),
-        pltpu.make_async_copy(jac_in, jac_ref, sem.at[23]),
-        pltpu.make_async_copy(inv_in, inv_ref, sem.at[24]),
+        pltpu.make_async_copy(inv_in, inv_ref, sem.at[23]),
     ]
     copies = [
         pltpu.make_async_copy(rend_in, rend_hbm, sem.at[0]),
@@ -588,23 +592,7 @@
         copy.start()
     for load in loads:
         load.wait()
-    du, dr, da, db, dc, do, *dcol = [grad_ref[pl.ds(f, 8, stride=16), :] for f in range(9)]
-    jac = [jac_ref[n] for n in range(62)]
-    conic = (da, db, dc)
-    geo = [sum(conic[i] * jac[i * 10 + n] for i in range(3)) for n in range(10)]
-    for n in range(3):
-        geo[n] = geo[n] + sum(dcol[ch] * jac[30 + ch * 3 + n] for ch in range(3))
-    ja, jx, jy, d_opaque = jac[39:43]
-    geo[0] = geo[0] + du * ja
-    geo[1] = geo[1] + dr * ja
-    geo[2] = geo[2] + du * jx + dr * jy
-    passed = [dcol[ch] * jac[43 + ch] for ch in range(3)]
-    rows = [passed[ch] * jac[46 + i] for ch in range(3) for i in range(16)] + geo + [do * d_opaque]
-    for i in range(59):
-        rows_ref[i * 8 : (i + 1) * 8, :] = rows[i]
-    for i in range(59, 64):
-        rows_ref[i * 8 : (i + 1) * 8, :] = jnp.zeros((8, 128), F32)
-    halves = [sum(rows_ref[pl.ds(v * 2 + j, 64, stride=8), :] for v in range(4)) for j in range(2)]
+    halves = [grad_ref[j] for j in range(2)]
     count = har_hbm.shape[1]
     pieces = 4
     wide = count // pieces
@@ -646,17 +634,16 @@
         return jax.ShapeDtypeStruct(dims, F32)
 
     params = [VMEM((48, count), F32), VMEM((3, count), F32), VMEM((3, count), F32), VMEM((4, count), F32), VMEM((1, count), F32)]
-    rendered, inverse_depth, jacobian, inverse, grads = pl.pallas_call(
+    rendered, inverse_depth, inverse, grads = pl.pallas_call(
         functools.partial(step_kernel, height, columns),
         out_shape=[
             shape(3, 16, 128),
             shape(16, 128),
-            shape(62, 8, 128),
             jax.ShapeDtypeStruct((32, 128), jnp.int32),
-            shape(128, 128),
+            shape(2, 64, 128),
         ],
         in_specs=[hbm] * 10,
-        out_specs=[hbm] * 5,
+        out_specs=[hbm] * 4,
         scratch_shapes=params + [
             VMEM((4, 3), F32),
             VMEM((2, 128), jnp.int32),
@@ -668,9 +655,9 @@
             VMEM((128, 128), F32),
             VMEM((32, 4, 128), F32),
             VMEM((32, 4, 128), F32),
-            VMEM((16, 8, 128), F32),
-            VMEM((16, 8, 128), F32),
-            VMEM((9, 256, 128), BF16),
+            VMEM((16, 5, 128), F32),
+            VMEM((16, 5, 128), F32),
+            VMEM((128, 2304), BF16),
             VMEM((6, 16, 128), F32),
             VMEM((6, 16, 128), F32),
             VMEM((16, 128, 128), F32),
@@ -682,13 +669,15 @@
             VMEM((4, 16, 128), F32),
             VMEM((3, 16, 128), F32),
             VMEM((12, 128, 128), F32),
-            VMEM((16, 8, 128), F32),
-            VMEM((16, 8, 128), F32),
+            VMEM((16, 5, 128), F32),
+            VMEM((16, 5, 128), F32),
             VMEM((32, 4, 128), F32),
             VMEM((32, 4, 128), F32),
-            VMEM((62, 8, 128), F32),
             VMEM((32, 128), jnp.int32),
-            dma((15,)),
+            VMEM((512, 128), F32),
+            VMEM((2, 64, 128), F32),
+            VMEM((128, 128), F32),
+            dma((14,)),
             dma((6,)),
             dma((6,)),
         ],
@@ -714,19 +703,17 @@
             shape(48, count), shape(3, count), shape(3, count), shape(4, count), shape(1, count),
             shape(3, 16, 128), shape(16, 128),
         ],
-        in_specs=[hbm] * 5,
+        in_specs=[hbm] * 4,
         out_specs=[hbm] * 7,
         scratch_shapes=[
-            VMEM((128, 128), F32),
-            VMEM((62, 8, 128), F32),
+            VMEM((2, 64, 128), F32),
             VMEM((32, 128), jnp.int32),
-            VMEM((512, 128), F32),
         ]
         + params
-        + [dma((25,))],
+        + [dma((24,))],
         compiler_params=pltpu.CompilerParams(vmem_limit_bytes=60 * 2**20),
         name="owner_pull",
-    )(grads, jacobian, inverse, rendered, inverse_depth)
+    )(grads, inverse, rendered, inverse_depth)
     return (
         rendered[None],
         inverse_depth[None],

time: 54.4 us -> 51.4 us (0.945)
  Pallas kernels: 53.6 us -> 50.6 us
    pallas_call x1, Pallas kernels: 50.9 us -> 48.1 us  [on_device(): pl.pallas_call(functools.partial(step_kernel, height, columns), out_shape...]
where the time goes in v3:
time: 51.4 us; the launch traced here: 51.2 us
  Pallas kernels  50.6 us (98%)
  between operations  0.64 us (1%)
    pallas_call x1, Pallas kernels, on_device(): pl.pallas_call(functools.partial(step_kernel, height, columns), out_shape...  48.1 us
    pallas_call x1, Pallas kernels, on_device(): pl.pallas_call(owner_kernel, out_shape=[shape(48, count), shape(3, count)...  2.46 us

profile of v3, /device:TPU:1, one launch (start us, length us, event | category | flops | bytes accessed | tf_op | source)
XLA Modules:
  0.0 51.2 jit_solution(3872062697512379530)
XLA Ops:
  0.6 48.1 %render_step.1 = (f32[3,16,128]{2,1,0:T(8,128)}, f32[16,128]{1,0:T(8,128)}, s32[32,128]{1,0:T(8,128)}, f32[2,64,128]{2,1,0:T(8,128)}) custom-call(f32[48,4096]{1,0:T(8,128)} %bitcast.11, f32[3,4096]{1,0:T(4,128)} %cen_hbm.1, f32[3,4096]{1,0:T(4,128)} %lsc_hbm.1, f32[4,4096]{1,0:T(4,128)} %rot_hbm.1, f32[1,4096]{1,0:T(1,128)} %bitcast.13, f32[4,3]{1,0:T(4,128)} %cam_hbm.1, ...), custom_call_target="tpu_custom_call" | custom-call | tf_op jit(solution)/shard_map/render_step/pallas_call | solution.py:637
  48.8 2.5 %owner_pull.1 = (f32[48,4096]{1,0:T(8,128)}, f32[3,4096]{1,0:T(4,128)}, f32[3,4096]{1,0:T(4,128)}, f32[4,4096]{1,0:T(4,128)}, f32[1,4096]{1,0:T(1,128)}, /*index=5*/f32[3,16,128]{2,1,0:T(8,128)}, f32[16,128]{1,0:T(8,128)}) custom-call(f32[2,64,128]{2,1,0:T(8,128)} %get-tuple-element.18.grad_in, s32[32,128]{1,0:T(8,128)} %get-tuple-element.19.inv_in, ...), custom_call_target="tpu_custom_call" | custom-call | tf_op jit(solution)/shard_map/owner_pull/pallas_call | solution.py:700

commit v4 on v3

--- a/solution.py
+++ b/solution.py
@@ -174,7 +174,7 @@
     rend_hbm, depth_hbm, inv_hbm, grad_hbm,
     har_ref, cen_ref, lsc_ref, rot_ref, opa_ref, cam_ref, idx_ref, list_ref, cnt_ref, target_ref,
     small, feat, sq, send1, recv1, send2, recv2, fold,
-    halo_x, halo_y, raws, trans, weights, dweights, xsplit, acc, image, gimage, fsc,
+    halo_x, halo_y, raws, trans, weights, dweights, xsplit, image, gimage, fsc,
     back2s, back2r, back1s, back1r, inv_ref, rows_ref, grad_ref, turn, lsem, ssem, rsem,
 ):
     s = lax.axis_index("space")
@@ -199,6 +199,9 @@
         z2 = lax.rem(z + d, 16)
         depth_peers.append((z2, (x * 32 + z2 * 2 + c, y)))
 
+    barrier = pltpu.get_barrier_semaphore()
+    for _, dev in depth_peers:
+        pl.semaphore_signal(barrier, inc=1, device_id=dev, device_id_type=MESH)
     pairs = (
         (har_hbm, har_ref), (idx_hbm, idx_ref), (cen_hbm, cen_ref), (lsc_hbm, lsc_ref), (rot_hbm, rot_ref),
         (opa_hbm, opa_ref), (cam_hbm, cam_ref), (list_hbm, list_ref), (cnt_hbm, cnt_ref), (target_hbm, target_ref),
@@ -206,9 +209,9 @@
     loads = [pltpu.make_async_copy(a, b, lsem.at[n]) for n, (a, b) in enumerate(pairs)]
     for load in loads:
         load.start()
-    barrier = pltpu.get_barrier_semaphore()
-    for _, dev in depth_peers + ring_peers + [(0, (lax.rem(s + 2 * c + 127, 128), y))]:
+    for _, dev in ring_peers + [(0, (lax.rem(s + 2 * c + 127, 128), y))]:
         pl.semaphore_signal(barrier, inc=1, device_id=dev, device_id_type=MESH)
+
     feat[...] = jnp.zeros_like(feat)
     small[...] = jnp.zeros_like(small)
 
@@ -441,7 +444,7 @@
         b_mx, b_xx, b_xy = (flat[(i * 3 + n) * 16 : (i * 3 + n + 1) * 16] for i in range(3))
         gimage[n] = b_mx + 2.0 * vx * b_xx + vy * b_xy + smooth
 
-    acc[...] = jnp.zeros_like(acc)
+    sums = [0.0] * 6
     for i in range(4):
         dws, products = [], []
         for row in range(i * 4, i * 4 + 4):
@@ -449,7 +452,6 @@
             dws.append(dw)
             products.append(jnp.concatenate(split(dw * weights[row], 2), axis=0))
         later = dot(upper, jnp.concatenate(products, axis=1))
-        sums = [0.0] * 6
         for n in range(4):
             row = i * 4 + n
             d_power = dws[n] * trans[row] - later[:, n * 128 : (n + 1) * 128] * raws[row]
@@ -458,9 +460,7 @@
             terms = [d_power, moved, moved * dy]
             terms += [weights[row] * gimage[f, row : row + 1, :] for f in range(3)]
             sums = [a + b for a, b in zip(sums, terms)]
-        for n in range(6):
-            acc[n] += sums[n]
-    s0, s1, s2 = acc[0], acc[1], acc[2]
+    s0, s1, s2 = sums[0:3]
     adx, cb, dx = fsc[9], fsc[10], fsc[11]
     grads = [
         -(adx * s0 + cb * s1),
@@ -469,9 +469,9 @@
         -dx * s1,
         -0.5 * s2,
         s0 / fsc[4],
-        acc[3],
-        acc[4],
-        acc[5],
+        sums[3],
+        sums[4],
+        sums[5],
     ]
     parts = [part for f in range(9) for part in split(grads[f], 2)]
     turned = lax.dot_general(
@@ -535,16 +535,18 @@
         send(back1s, at, back1r, me, 5, dev)
     back1r[me] = back1s[me]
     wait_bytes(back1r, 31, rsem.at[5])
-    for a in range(8):
-        first = (a // 2) * 32 + a % 2
-        rows = [back1r[v * 8 + a] for v in range(4)]
+    for a in range(4):
+        rows = [
+            jnp.concatenate([back1r[v * 8 + 2 * a], back1r[v * 8 + 2 * a + 1]], axis=0) for v in range(4)
+        ]
         for z4 in range(4):
             out = rows[z4]
             for v in range(4):
                 if v != z4:
                     moved = pltpu.roll(rows[v], ((v - z4) * 32) % 128, axis=1)
-                    out = jnp.where(quarter[0:4] == v, moved, out)
-            sq[pl.ds(first + z4 * 2, 4, stride=8), :] = out
+                    out = jnp.where(quarter == v, moved, out)
+            for n in range(2):
+                sq[pl.ds(a * 32 + n + z4 * 2, 4, stride=8), :] = out[n * 4 : n * 4 + 4]
     turn[...] = jnp.transpose(sq[...])
     du, dr, da, db, dc, do, *dcol = [turn[pl.ds(SEAT[f], 8, stride=16), :] for f in range(9)]
     conic = (da, db, dc)
@@ -582,7 +584,7 @@
 ):
     loads = [
         pltpu.make_async_copy(grad_in, grad_ref, sem.at[22]),
-        pltpu.make_async_copy(inv_in, inv_ref, sem.at[23]),
+        pltpu.make_async_copy(inv_in, inv_ref, sem.at[43]),
     ]
     copies = [
         pltpu.make_async_copy(rend_in, rend_hbm, sem.at[0]),
@@ -594,7 +596,7 @@
         load.wait()
     halves = [grad_ref[j] for j in range(2)]
     count = har_hbm.shape[1]
-    pieces = 4
+    pieces = 8
     wide = count // pieces
     for piece in range(pieces):
         for h in range(piece * wide // 128, (piece + 1) * wide // 128):
@@ -665,7 +667,6 @@
             VMEM((16, 128, 128), F32),
             VMEM((16, 128, 128), F32),
             VMEM((256, 2048), BF16),
-            VMEM((6, 128, 128), F32),
             VMEM((4, 16, 128), F32),
             VMEM((3, 16, 128), F32),
             VMEM((12, 128, 128), F32),
@@ -710,7 +711,7 @@
             VMEM((32, 128), jnp.int32),
         ]
         + params
-        + [dma((24,))],
+        + [dma((44,))],
         compiler_params=pltpu.CompilerParams(vmem_limit_bytes=60 * 2**20),
         name="owner_pull",
     )(grads, inverse, rendered, inverse_depth)

time: 51.4 us -> 51.5 us (level)
  no operation moved by 1% of the time
where the time goes in v4:
time: 51.5 us; the launch traced here: 51.4 us
  Pallas kernels  50.7 us (98%)
  between operations  0.64 us (1%)
    pallas_call x1, Pallas kernels, on_device(): pl.pallas_call(functools.partial(step_kernel, height, columns), out_shape...  48.1 us
    pallas_call x1, Pallas kernels, on_device(): pl.pallas_call(owner_kernel, out_shape=[shape(48, count), shape(3, count)...  2.6 us

profile of v4, /device:TPU:1, one launch (start us, length us, event | category | flops | bytes accessed | tf_op | source)
XLA Modules:
  0.0 51.4 jit_solution(16218830252298797335)
XLA Ops:
  0.6 48.1 %render_step.1 = (f32[3,16,128]{2,1,0:T(8,128)}, f32[16,128]{1,0:T(8,128)}, s32[32,128]{1,0:T(8,128)}, f32[2,64,128]{2,1,0:T(8,128)}) custom-call(f32[48,4096]{1,0:T(8,128)} %bitcast.11, f32[3,4096]{1,0:T(4,128)} %cen_hbm.1, f32[3,4096]{1,0:T(4,128)} %lsc_hbm.1, f32[4,4096]{1,0:T(4,128)} %rot_hbm.1, f32[1,4096]{1,0:T(1,128)} %bitcast.13, f32[4,3]{1,0:T(4,128)} %cam_hbm.1, ...), custom_call_target="tpu_custom_call" | custom-call | tf_op jit(solution)/shard_map/render_step/pallas_call | solution.py:639
  48.7 2.6 %owner_pull.1 = (f32[48,4096]{1,0:T(8,128)}, f32[3,4096]{1,0:T(4,128)}, f32[3,4096]{1,0:T(4,128)}, f32[4,4096]{1,0:T(4,128)}, f32[1,4096]{1,0:T(1,128)}, /*index=5*/f32[3,16,128]{2,1,0:T(8,128)}, f32[16,128]{1,0:T(8,128)}) custom-call(f32[2,64,128]{2,1,0:T(8,128)} %get-tuple-element.18.grad_in, s32[32,128]{1,0:T(8,128)} %get-tuple-element.19.inv_in, ...), custom_call_target="tpu_custom_call" | custom-call | tf_op jit(solution)/shard_map/owner_pull/pallas_call | solution.py:701
